TPU v7x, 1024 devices: a whole 4x4x32 slice. The times are simulated.
1024 devices in a mesh: gx: 32 (over z), gy: 8 (over y, core), gz: 4 (over x).
Axes of the slice: x: 4, y: 4, z: 32, core: 2. Of those that a mesh axis runs over, the one named last changes fastest.
Arguments:
- stiff_blocks: bfloat16 [128, 16, 4, 4, 192, 192], P('gx', 'gy', 'gz'), may hold values from -6 to 6
- stiff_cols: int32 [128, 16, 4, 4], P('gx', 'gy', 'gz'), may hold values from 0 to 8191, as said below
- prolong_blocks: bfloat16 [128, 16, 4, 4, 6, 192], P('gx', 'gy', 'gz'), may hold values from -0.4375 to 0.4375
- prolong_cols: int32 [128, 16, 4, 4], P('gx', 'gy', 'gz'), may hold values from 0 to 8191, as said below
- agg_nodes: int32 [128, 16, 4], P('gx', 'gy', 'gz'), may hold values from 32 to 64
- row_owner: int32 [32, 8, 4, 8, 1], P('gx', None, 'gz'), may hold values from 0 to 7; in each aligned block of 8 rows (0 to 7, 8 to 15, ..., all dimensions but the last counted through in order) at most 2 rows name the same one
Outputs:
- coarse_owned: float32 [32, 64, 4, 2, 2268], P('gx', 'gy', 'gz')
Inputs may be any that keep to these rules, and one draw needn't show every extreme that they name: `stiff_cols`: entry 0 is the aggregate's own id; the other 3 are distinct aggregates sharing a face with it. `prolong_cols`: entry 0 is the aggregate's own id; the other 3 are distinct aggregates sharing a face with it. `row_owner`: within the 8 rows of one block no rank is named more than 2 times, and in some blocks one rank is named exactly 2 times.
All inputs are finite; a program needn't handle non-finite values.
Results may differ from a plain program's by a relative error of at most 0.0029.
Values may be sent and summed in bfloat16 or wider, within the bound.
A program may use at most 32 MiB of HBM per device.

v0:
```python
import jax
import jax.numpy as jnp
import numpy as np
from jax import lax
from jax.sharding import PartitionSpec as P


def padded_2(block, sides, width):
    for axis, dim in sides:
        count = lax.axis_size(axis)
        forward = [(i, i + 1) for i in range(count - 1)]
        backward = [(target, source) for source, target in forward]
        low = lax.ppermute(
            lax.slice_in_dim(block, block.shape[dim] - width, None, axis=dim), axis, forward
        )
        high = lax.ppermute(lax.slice_in_dim(block, 0, width, axis=dim), axis, backward)
        block = jnp.concatenate([low, block, high], axis=dim)
    return block


def offset_points(radius):
    return [
        (step_x, step_y, step_z)
        for step_x in range(-radius, radius + 1)
        for step_y in range(-radius, radius + 1)
        for step_z in range(-radius, radius + 1)
        if abs(step_x) + abs(step_y) + abs(step_z) <= radius
    ]


def offset_table(radius):
    return np.array(offset_points(radius), dtype=np.int32)


def box_lookup(radius):
    side_len = 2 * radius + 1
    lookup = [0] * side_len**3
    for number, triple in enumerate(offset_points(radius)):
        code_at = (
            ((triple[0] + radius) * side_len + triple[1] + radius) * side_len + triple[2] + radius
        )
        lookup[code_at] = number
    return np.array(lookup, dtype=np.int32)


def box_index(offsets, radius):
    side_len = 2 * radius + 1
    shifted = offsets + radius
    return ((shifted[..., 0] * side_len + shifted[..., 1]) * side_len + shifted[..., 2]).astype(
        jnp.int32
    )


def decode_ids(agg_ids, whole_y, whole_z):
    return jnp.stack(
        [agg_ids // (whole_y * whole_z), agg_ids // whole_z % whole_y, agg_ids % whole_z], axis=-1
    )


def fold_axis(padded, axis_dim, core_len):
    core_part = lax.slice_in_dim(padded, 2, core_len + 2, axis=axis_dim)
    low_part = lax.slice_in_dim(padded, 0, 1, axis=axis_dim)
    high_part = lax.slice_in_dim(padded, core_len + 3, core_len + 4, axis=axis_dim)
    shape_one = [1] * padded.ndim
    shape_one[axis_dim] = core_len
    position = lax.broadcasted_iota(jnp.int32, tuple(shape_one), axis_dim)
    return (
        core_part
        + jnp.where(position == 0, low_part, 0.0)
        + jnp.where(position == core_len - 1, high_part, 0.0)
    )


def local(stiff_blocks, stiff_cols, prolong_blocks, prolong_cols, agg_nodes, row_owner):
    block_x, block_y, block_z, slot_a, row_count = stiff_blocks.shape[:5]
    slot_p, mode_count = (prolong_blocks.shape[3], prolong_blocks.shape[4])
    agg_count = block_x * block_y * block_z
    group_y = lax.axis_size("gy")
    whole_y = block_y * group_y
    whole_z = block_z * lax.axis_size("gz")
    anchor = jnp.stack(
        [
            lax.axis_index("gx") * block_x,
            lax.axis_index("gy") * block_y,
            lax.axis_index("gz") * block_z,
        ]
    )
    local_ids = jnp.arange(agg_count, dtype=jnp.int32)
    local_pos = jnp.stack(
        [local_ids // (block_y * block_z), local_ids // block_z % block_y, local_ids % block_z],
        axis=-1,
    )
    global_pos = local_pos + anchor
    live_rows = (
        lax.broadcasted_iota(jnp.int32, (block_x, block_y, block_z, row_count), 3)
        < 3 * agg_nodes[..., None]
    )
    p_live = jnp.where(
        live_rows[:, :, :, None, None, :], prolong_blocks, jnp.zeros((), jnp.bfloat16)
    )
    p_live = p_live.reshape(agg_count, slot_p, mode_count, row_count)
    p_delta = (
        decode_ids(prolong_cols.reshape(agg_count, slot_p), whole_y, whole_z)
        - global_pos[:, None, :]
    )
    face_dir = jnp.asarray(box_lookup(1))[box_index(p_delta, 1)]
    dir_onehot = (face_dir[..., None] == jnp.arange(7, dtype=jnp.int32)).astype(jnp.bfloat16)
    p_dense = jnp.einsum(
        "ntd,ntcr->ndcr", dir_onehot, p_live, preferred_element_type=jnp.float32
    ).astype(jnp.bfloat16)
    p_dense = p_dense.reshape(block_x, block_y, block_z, 7, mode_count, row_count)
    p_extended = padded_2(p_dense, (("gx", 0), ("gy", 1), ("gz", 2)), 1)
    ext_y = block_y + 2
    ext_z = block_z + 2
    p_table = p_extended.reshape(-1, 7, mode_count, row_count)
    a_delta = (
        decode_ids(stiff_cols.reshape(agg_count, slot_a), whole_y, whole_z) - global_pos[:, None, :]
    )
    a_place = local_pos[:, None, :] + a_delta + 1
    a_slot = (a_place[..., 0] * ext_y + a_place[..., 1]) * ext_z + a_place[..., 2]
    p_near = p_table[a_slot]
    stiff_flat = stiff_blocks.reshape(agg_count, slot_a, row_count, row_count)
    products = jnp.einsum(
        "nsrm,nsdcm->nsdcr", stiff_flat, p_near, preferred_element_type=jnp.float32
    )
    face_pts = jnp.asarray(offset_table(1))
    near_pts = jnp.asarray(offset_table(2))
    near_count = near_pts.shape[0]
    near_index = jnp.asarray(box_lookup(2))[box_index(a_delta[:, :, None, :] + face_pts, 2)]
    near_onehot = (near_index[..., None] == jnp.arange(near_count, dtype=jnp.int32)).astype(
        jnp.float32
    )
    ap_rows = jnp.einsum(
        "nsdo,nsdcr->nocr", near_onehot, products, precision=lax.Precision.HIGHEST
    ).astype(jnp.bfloat16)
    coarse_terms = jnp.einsum(
        "nuar,nocr->nuoac", p_live, ap_rows, preferred_element_type=jnp.float32
    )
    ball_count = offset_table(3).shape[0]
    mode_square = mode_count * mode_count
    ball_index = jnp.asarray(box_lookup(3))[
        box_index(near_pts[None, None, :, :] - p_delta[:, :, None, :], 3)
    ]
    target_place = local_pos[:, None, :] + p_delta + 1
    target_slot = (target_place[..., 0] * ext_y + target_place[..., 1]) * ext_z + target_place[
        ..., 2
    ]
    segment_ids = target_slot[..., None] * ball_count + ball_index
    ext_count = (block_x + 2) * ext_y * ext_z
    term_rows = coarse_terms.reshape(-1, mode_square)
    partial_value = jax.ops.segment_sum(
        term_rows, segment_ids.reshape(-1), num_segments=ext_count * ball_count
    )
    partial_value = partial_value.reshape(block_x + 2, ext_y, ext_z, ball_count * mode_square)
    pushed = padded_2(partial_value, (("gx", 0), ("gy", 1), ("gz", 2)), 1)
    folded = fold_axis(fold_axis(fold_axis(pushed, 0, block_x), 1, block_y), 2, block_z)
    coarse_rows = folded.reshape(agg_count, -1)
    capacity = max(2, (2 * agg_count + group_y - 1) // group_y)
    my_rank = lax.axis_index("gy")
    owners = row_owner[0, :, 0, :, 0]
    earlier = lax.broadcasted_iota(jnp.int32, (agg_count, agg_count), 1) < lax.broadcasted_iota(
        jnp.int32, (agg_count, agg_count), 0
    )
    rank_in = jnp.sum(
        ((owners[:, :, None] == owners[:, None, :]) & earlier).astype(jnp.int32), axis=2
    )
    slot_ids = jnp.arange(capacity, dtype=jnp.int32)
    pencil = lax.all_gather(coarse_rows[None], "gy", axis=0, tiled=True)
    selector = (
        (owners[:, None, :] == my_rank) & (rank_in[:, None, :] == slot_ids[None, :, None])
    ).astype(jnp.float32)
    delivered = jnp.einsum("scq,sql->scl", selector, pencil, precision=lax.Precision.HIGHEST)
    return delivered[None, :, None]


def solution(mesh):
    return jax.shard_map(
        local,
        mesh=mesh,
        in_specs=(
            P("gx", "gy", "gz", None, None, None),
            P("gx", "gy", "gz", None),
            P("gx", "gy", "gz", None, None, None),
            P("gx", "gy", "gz", None),
            P("gx", "gy", "gz"),
            P("gx", None, "gz", None, None),
        ),
        out_specs=P("gx", "gy", "gz", None, None),
        check_vma=False,
    )
```

profile of v0, /device:TPU:1, one launch (start us, length us, event | category | flops | bytes accessed | tf_op | source)
XLA Modules:
  0.0 135.3 jit_solution(18051397192775177309)
XLA Ops:
  0.0 0.9 add_select_fusion.3
  1.3 0.7 gather_fusion.2
  2.3 0.3 convolution_convert_fusion
  2.7 0.7 copy-done.4
  3.3 0.6 slice_bitcast_fusion.2
  4.0 5.0 %collective-permute-start = (bf16[1,2,1,7,6,192]{5,3,4,1,2,0:T(8,128)(2,1)S(1)}, bf16[1,2,1,7,6,192]{5,3,4,1,2,0:T(8,128)(2,1)}, u32[]{:S(2)}, u32[]{:S(2)}) collective-permute-start(bf16[1,2,1,7,6,192]{5,3,4,1,2,0:T(8,128)(2,1)S(1)} %get-tuple-element.22), channel_id=1, source_target_pairs={{0,32},{32,64},{64,96},{96,128},{128,160},{160,192},{192,224},{224... | collective-permute-start | bytes 96776 | tf_op jit(solution)/shard_map/ppermute | solution.py:13
  8.9 1.3 collective-permute-start.1
  10.2 0.6 compare_select_fusion.2
  11.1 0.6 fusion.27
  11.7 0.7 reshape.640
  12.4 0.7 reshape.632
  13.1 0.8 copy_dynamic-update-slice_fusion.2
  13.9 1.1 copy_dynamic-update-slice_fusion
  15.1 0.4 fusion.36
  15.5 4.1 %collective-permute-start.2 = (bf16[6,1,1,7,6,192]{5,1,4,3,2,0:T(2,128)(2,1)S(1)}, bf16[6,1,1,7,6,192]{5,1,4,3,2,0:T(2,128)(2,1)S(1)}, u32[]{:S(2)}, u32[]{:S(2)}) collective-permute-start(bf16[6,1,1,7,6,192]{5,1,4,3,2,0:T(2,128)(2,1)S(1)} %get-tuple-element.19), channel_id=1, source_target_pairs={{0,4},{4,8},{8,12},{12,16},{16,20},{20,24},{24,28},{1,5},{5,9},{9,... | collective-permute-start | bytes 290312 | tf_op jit(solution)/shard_map/ppermute | solution.py:13
  19.6 10.2 %collective-permute-start.3 = (bf16[6,1,1,7,6,192]{5,1,4,3,2,0:T(2,128)(2,1)S(1)}, bf16[6,1,1,7,6,192]{5,1,4,3,2,0:T(2,128)(2,1)S(1)}, u32[]{:S(2)}, u32[]{:S(2)}) collective-permute-start(bf16[6,1,1,7,6,192]{5,1,4,3,2,0:T(2,128)(2,1)S(1)} %get-tuple-element.20), channel_id=1, source_target_pairs={{4,0},{8,4},{12,8},{16,12},{20,16},{24,20},{28,24},{5,1},{9,5},{13... | collective-permute-start | bytes 290312 | tf_op jit(solution)/shard_map/ppermute | solution.py:16
  29.8 0.7 pad_clamp_fusion.2
  30.5 0.5 collective-permute-done.3
  31.0 0.2 copy-done.5
  31.2 1.8 %pad_maximum_fusion.2 = bf16[6,4,1,7,6,192]{5,1,4,3,2,0:T(4,128)(2,1)} fusion(bf16[6,1,1,7,6,192]{5,1,4,3,2,0:T(2,128)(2,1)S(1)} %collective-permute-done.3, bf16[6,2,1,7,6,192]{5,1,4,3,2,0:T(2,128)(2,1)S(1)} %copy_dynamic-update-slice_fusion.1, bf16[6,1,1,7,6,192]{5,1,4,3,2,0:T(2,128)(2,1)S(1)} %collective-permute-done.2), kind=kLoop, calls=%fused_computation.20 | loop fusion | flops 1161216 | bytes 774144 | tf_op jit(solution)/shard_map/concatenate | solution.py:17
  33.0 2.1 %collective-permute-start.4 = (bf16[6,4,1,7,6,192]{5,1,4,3,2,0:T(4,128)(2,1)}, bf16[6,4,1,7,6,192]{5,1,4,3,2,0:T(4,128)(2,1)}, u32[]{:S(2)}, u32[]{:S(2)}) collective-permute-start(bf16[6,4,1,7,6,192]{5,1,4,3,2,0:T(4,128)(2,1)} %pad_maximum_fusion.2), channel_id=1, source_target_pairs={{0,1},{1,2},{2,3},{4,5},{5,6},{6,7},{8,9},{9,10},{10,11},{12,13},{... | collective-permute-start | bytes 1161224 | tf_op jit(solution)/shard_map/ppermute | solution.py:13
  35.1 1.3 collective-permute-start.5
  36.5 1.9 %gather_fusion.1 = s32[224]{0:T(256)S(1)} fusion(s32[125]{0:T(128)S(1)} %copy-done.1, s32[1024]{0:T(1024)S(1)} %pad_clamp_fusion.2), kind=kCustom, calls=%fused_computation.1 | custom fusion | bytes 2688 | tf_op jit(solution)/shard_map/gather | solution.py:129
  38.5 0.6 copy-done.2
  39.0 5.4 %gather_fusion = s32[800]{0:T(1024)S(1)} fusion(s32[343]{0:T(512)S(1)} %copy-done.2, s32[1024]{0:T(1024)S(1)} %pad_clamp_fusion.3), kind=kCustom, calls=%fused_computation | custom fusion | bytes 9600 | tf_op jit(solution)/shard_map/gather | solution.py:141
  44.6 0.7 broadcast_add_fusion
  45.3 0.8 reshape.664
  46.1 4.3 %collective-permute-done.5 = bf16[6,4,1,7,6,192]{5,1,4,3,2,0:T(4,128)(2,1)} collective-permute-done((bf16[6,4,1,7,6,192]{5,1,4,3,2,0:T(4,128)(2,1)}, bf16[6,4,1,7,6,192]{5,1,4,3,2,0:T(4,128)(2,1)}, u32[]{:S(2)}, u32[]{:S(2)}) %collective-permute-start.5) | collective-permute-done | bytes 387104 | tf_op jit(solution)/shard_map/ppermute | solution.py:16
  50.5 2.9 %pad_maximum_fusion.1 = bf16[6,4,3,7,6,192]{5,1,4,3,2,0:T(4,128)(2,1)S(1)} fusion(bf16[6,4,1,7,6,192]{5,1,4,3,2,0:T(4,128)(2,1)} %collective-permute-done.5, bf16[6,1,1,7,6,192]{5,1,4,3,2,0:T(2,128)(2,1)} %copy-done.6, bf16[6,2,1,7,6,192]{5,1,4,3,2,0:T(2,128)(2,1)S(1)} %copy_dynamic-update-slice_fusion.1, bf16[6,1,1,7,6,192]{5,1,4,3,2,0:T(2,128)(2,1)} %copy-done.5, ...), kind=kLoop, calls=%fused_computation.10 | loop fusion | flops 5806080 | bytes 2322432 | tf_op jit(solution)/shard_map/concatenate | solution.py:17
  53.3 1.6 %copy.62 = bf16[6,4,3,7,6,192]{5,3,4,2,1,0:T(8,128)(2,1)} copy(bf16[6,4,3,7,6,192]{5,1,4,3,2,0:T(4,128)(2,1)S(1)} %pad_maximum_fusion.1) | data formatting | bytes 2322432 | tf_op jit(solution)/shard_map/concatenate | solution.py:17
  55.0 3.0 %gather_fusion.3 = bf16[32,7,6,192]{3,1,2,0:T(8,128)(2,1)} fusion(bf16[72,7,6,192]{3,1,2,0:T(8,128)(2,1)} %bitcast.74, s32[1024]{0:T(1024)S(1)} %pad_clamp_fusion), kind=kCustom, calls=%fused_computation.3 | custom fusion | bytes 1032320 | tf_op jit(solution)/shard_map/gather | solution.py:121
  58.0 2.2 %fusion.4 = f32[8,4,7,6,192]{4,2,1,3,0:T(8,128)S(1)} fusion(bf16[8,4,192,192,1]{3,2,1,4,0:T(8,128)(2,1)S(1)} %bitcast.73, bf16[8,4,7,6,192]{4,2,3,1,0:T(8,128)(2,1)} %bitcast.75), kind=kOutput, calls=%fused_computation.16 | convolution fusion | flops 99090432 | bytes 3907584 | tf_op jit(solution)/shard_map/nsrm,nsdcm->nsdcr/dot_general | solution.py:123
  60.2 1.2 fusion.1
  61.4 0.7 convolution_bitcast_fusion.1
  62.1 1.0 copy.66
  63.1 1.6 %reshape.666 = f32[800,36]{0,1:T(8,128)S(1)} reshape(f32[8,4,25,6,6]{2,1,0,4,3:T(4,128)} %copy.66) | data formatting | bytes 230400 | tf_op jit(solution)/shard_map/reshape | solution.py:150
  64.7 1.0 copy.67
  65.6 7.9 %scatter_custom_fusion = f32[4536,36]{1,0:T(8,128)} fusion(s32[800]{0:T(1024)S(1)} %reshape.664, f32[800,36]{1,0:T(8,128)} %copy.67, f32[]{:T(128)} %constant.155.clone.1), kind=kCustom, calls=%fused_computation.14 | custom fusion | flops 28800 | bytes 653696 | tf_op jit(solution)/shard_map/scatter-add | solution.py:151
  73.6 1.9 %fusion.34 = (f32[756,36]{1,0:T(8,128)S(1)}, f32[756,36]{1,0:T(8,128)}) fusion(f32[4536,36]{1,0:T(8,128)} %scatter_custom_fusion), kind=kLoop, calls=%fused_computation.138 | loop fusion | bytes 435456 | tf_op jit(solution)/shard_map/slice | solution.py:16
  75.5 1.9 %slice.136 = f32[1,4,3,2268]{3,2,1,0:T(4,128)} reshape(f32[756,36]{1,0:T(8,128)} %get-tuple-element.12) | data formatting | bytes 217728 | tf_op jit(solution)/shard_map/slice | solution.py:14
  77.4 4.9 %collective-permute-start.6 = (f32[1,4,3,2268]{3,2,1,0:T(4,128)}, f32[1,4,3,2268]{3,2,1,0:T(4,128)}, u32[]{:S(2)}, u32[]{:S(2)}) collective-permute-start(f32[1,4,3,2268]{3,2,1,0:T(4,128)} %slice.136), channel_id=1, source_target_pairs={{0,32},{32,64},{64,96},{96,128},{128,160},{160,192},{192,224},{224... | collective-permute-start | bytes 326600 | tf_op jit(solution)/shard_map/ppermute | solution.py:13
  82.2 3.5 %reshape.629 = f32[6,4,3,2268]{3,2,1,0:T(4,128)} reshape(f32[4536,36]{1,0:T(8,128)} %scatter_custom_fusion) | data formatting | bytes 1306368 | tf_op jit(solution)/shard_map/reshape | solution.py:154
  85.7 0.9 slice.138
  86.6 1.3 collective-permute-start.7
  87.9 0.9 constant_dynamic-update-slice_fusion.2
  88.8 1.4 %constant_dynamic-update-slice_fusion.1 = f32[8,4,3,2268]{3,2,1,0:T(4,128)S(1)} fusion(f32[8,4,3,2268]{3,2,1,0:T(4,128)S(1)} %constant_dynamic-update-slice_fusion.2, f32[6,4,3,2268]{3,2,1,0:T(4,128)} %reshape.629), kind=kLoop, calls=%fused_computation.60 | loop fusion | bytes 1537920
  90.2 2.5 %collective-permute-done.7 = f32[1,4,3,2268]{3,2,1,0:T(4,128)S(1)} collective-permute-done((f32[1,4,3,2268]{3,2,1,0:T(4,128)}, f32[1,4,3,2268]{3,2,1,0:T(4,128)S(1)}, u32[]{:S(2)}, u32[]{:S(2)}) %collective-permute-start.7) | collective-permute-done | bytes 108896 | tf_op jit(solution)/shard_map/ppermute | solution.py:16
  92.9 2.9 %collective-permute-start.8 = (f32[8,1,3,2268]{3,2,1,0:T(4,128)S(1)}, f32[8,1,3,2268]{3,2,1,0:T(4,128)S(1)}, u32[]{:S(2)}, u32[]{:S(2)}) collective-permute-start(f32[8,1,3,2268]{3,2,1,0:T(4,128)S(1)} %get-tuple-element.17), channel_id=1, source_target_pairs={{0,4},{4,8},{8,12},{12,16},{16,20},{20,24},{24,28},{1,5},{5,9},{9,... | collective-permute-start | bytes 653192 | tf_op jit(solution)/shard_map/ppermute | solution.py:13
  95.7 2.7 %collective-permute-start.9 = (f32[8,1,3,2268]{3,2,1,0:T(4,128)S(1)}, f32[8,1,3,2268]{3,2,1,0:T(4,128)S(1)}, u32[]{:S(2)}, u32[]{:S(2)}) collective-permute-start(f32[8,1,3,2268]{3,2,1,0:T(4,128)S(1)} %get-tuple-element.18), channel_id=1, source_target_pairs={{4,0},{8,4},{12,8},{16,12},{20,16},{24,20},{28,24},{5,1},{9,5},{13... | collective-permute-start | bytes 653192 | tf_op jit(solution)/shard_map/ppermute | solution.py:16
  98.5 0.9 collective-permute-done.8
  99.4 4.4 %collective-permute-done.9 = f32[8,1,3,2268]{3,2,1,0:T(4,128)S(1)} collective-permute-done((f32[8,1,3,2268]{3,2,1,0:T(4,128)S(1)}, f32[8,1,3,2268]{3,2,1,0:T(4,128)S(1)}, u32[]{:S(2)}, u32[]{:S(2)}) %collective-permute-start.9) | collective-permute-done | bytes 217760 | tf_op jit(solution)/shard_map/ppermute | solution.py:16
  103.8 0.7 pad_maximum_fusion.5
  104.5 2.4 %collective-permute-start.10 = (f32[8,6,1,2268]{3,2,1,0:T(1,128)S(1)}, f32[8,6,1,2268]{3,2,1,0:T(1,128)S(1)}, u32[]{:S(2)}, u32[]{:S(2)}) collective-permute-start(f32[8,6,1,2268]{3,2,1,0:T(1,128)S(1)} %get-tuple-element.15), channel_id=1, source_target_pairs={{0,1},{1,2},{2,3},{4,5},{5,6},{6,7},{8,9},{9,10},{10,11},{12,13},{... | collective-permute-start | bytes 1306376 | tf_op jit(solution)/shard_map/ppermute | solution.py:13
  106.8 1.3 collective-permute-start.11
  108.2 0.3 convert_reduce_fusion
  108.5 4.2 %collective-permute-done.10 = f32[8,6,1,2268]{3,2,1,0:T(1,128)S(1)} collective-permute-done((f32[8,6,1,2268]{3,2,1,0:T(1,128)S(1)}, f32[8,6,1,2268]{3,2,1,0:T(1,128)S(1)}, u32[]{:S(2)}, u32[]{:S(2)}) %collective-permute-start.10) | collective-permute-done | bytes 435488 | tf_op jit(solution)/shard_map/ppermute | solution.py:13
  112.7 4.1 %collective-permute-done.11 = f32[8,6,1,2268]{3,2,1,0:T(1,128)S(1)} collective-permute-done((f32[8,6,1,2268]{3,2,1,0:T(1,128)S(1)}, f32[8,6,1,2268]{3,2,1,0:T(1,128)S(1)}, u32[]{:S(2)}, u32[]{:S(2)}) %collective-permute-start.11) | collective-permute-done | bytes 435488 | tf_op jit(solution)/shard_map/ppermute | solution.py:16
  116.8 0.3 maximum_bitcast_fusion.1
  117.1 1.1 pad_maximum_fusion
  118.3 0.3 fusion
  118.6 0.2 fusion.6
  118.8 0.1 slice_add_fusion.2
  118.9 15.3 %all_gather.3 = f32[8,8,2268]{2,1,0:T(8,128)S(1)} all-gather(f32[1,8,2268]{2,1,0:T(8,128)S(1)} %copy.68), channel_id=1, replica_groups=mesh['gx'=32,'gy'=8,'gz'=4] {'gy'}, dimensions={0}, use_global_device_ids=true | all-gather | bytes 653184 | tf_op jit(solution)/shard_map/all_gather | solution.py:168
  134.3 1.1 convolution_bitcast_fusion
  (64 shorter events, 1.6 us)
Async XLA Ops:
  0.0 58.0 %copy-start = (bf16[4,2,1,4,192,192]{5,4,3,2,1,0:T(8,128)(2,1)S(1)}, bf16[4,2,1,4,192,192]{5,4,3,2,1,0:T(8,128)(2,1)}, u32[]{:S(2)}) copy-start(bf16[4,2,1,4,192,192]{5,4,3,2,1,0:T(8,128)(2,1)} %param.11) | copy-start | bytes 7077892
  0.0 1.2 copy-start.3
  1.2 0.8 copy-start.14
  1.3 1.0 copy-start.7
  1.3 9.6 %copy-start.13 = (s32[7,3]{0,1:T(4,128)S(1)}, s32[7,3]{0,1:T(4,128)}, u32[]{:S(2)}) copy-start(s32[7,3]{0,1:T(4,128)} %constant.176.clone) | copy-start | bytes 256
  1.3 9.7 %copy-start.12 = (s32[25,3]{0,1:T(4,128)S(1)}, s32[25,3]{0,1:T(4,128)}, u32[]{:S(2)}) copy-start(s32[25,3]{0,1:T(4,128)} %constant.177.clone) | copy-start | bytes 904
  2.7 0.7 copy-start.4
  3.3 33.1 %copy-start.1 = (s32[125]{0:T(128)S(1)}, s32[125]{0:T(128)}, u32[]{:S(2)}) copy-start(s32[125]{0:T(128)} %constant.178.clone) | copy-start | bytes 1504
  4.0 9.1 %collective-permute-start = (bf16[1,2,1,7,6,192]{5,3,4,1,2,0:T(8,128)(2,1)S(1)}, bf16[1,2,1,7,6,192]{5,3,4,1,2,0:T(8,128)(2,1)}, u32[]{:S(2)}, u32[]{:S(2)}) collective-permute-start(bf16[1,2,1,7,6,192]{5,3,4,1,2,0:T(8,128)(2,1)S(1)} %get-tuple-element.22), channel_id=1, source_target_pairs={{0,32},{32,64},{64,96},{96,128},{128,160},{160,192},{192,224},{224... | collective-permute-start | bytes 96776 | tf_op jit(solution)/shard_map/ppermute | solution.py:13
  8.9 6.1 %collective-permute-start.1 = (bf16[1,2,1,7,6,192]{5,3,4,1,2,0:T(8,128)(2,1)}, bf16[1,2,1,7,6,192]{5,3,4,1,2,0:T(8,128)(2,1)S(1)}, u32[]{:S(2)}, u32[]{:S(2)}) collective-permute-start(bf16[1,2,1,7,6,192]{5,3,4,1,2,0:T(8,128)(2,1)} %get-tuple-element.21), channel_id=1, source_target_pairs={{32,0},{64,32},{96,64},{128,96},{160,128},{192,160},{224,192},{256... | collective-permute-start | bytes 96776 | tf_op jit(solution)/shard_map/ppermute | solution.py:16
  13.1 23.3 %copy-start.9 = (s32[800]{0:T(1024)S(1)}, s32[800]{0:T(1024)}, u32[]{:S(2)}) copy-start(s32[800]{0:T(1024)} %reshape.632) | copy-start | bytes 9604
  15.1 21.3 %copy-start.11 = (s32[8,4,1]{1,0,2:T(8,128)S(1)}, s32[8,4,1]{1,0,2:T(8,128)}, u32[]{:S(2)}) copy-start(s32[8,4,1]{1,0,2:T(8,128)} %compare_select_fusion.2) | copy-start | bytes 388
  15.5 15.0 %collective-permute-start.2 = (bf16[6,1,1,7,6,192]{5,1,4,3,2,0:T(2,128)(2,1)S(1)}, bf16[6,1,1,7,6,192]{5,1,4,3,2,0:T(2,128)(2,1)S(1)}, u32[]{:S(2)}, u32[]{:S(2)}) collective-permute-start(bf16[6,1,1,7,6,192]{5,1,4,3,2,0:T(2,128)(2,1)S(1)} %get-tuple-element.19), channel_id=1, source_target_pairs={{0,4},{4,8},{8,12},{12,16},{16,20},{20,24},{24,28},{1,5},{5,9},{9,... | collective-permute-start | bytes 290312 | tf_op jit(solution)/shard_map/ppermute | solution.py:13
  19.6 11.4 %collective-permute-start.3 = (bf16[6,1,1,7,6,192]{5,1,4,3,2,0:T(2,128)(2,1)S(1)}, bf16[6,1,1,7,6,192]{5,1,4,3,2,0:T(2,128)(2,1)S(1)}, u32[]{:S(2)}, u32[]{:S(2)}) collective-permute-start(bf16[6,1,1,7,6,192]{5,1,4,3,2,0:T(2,128)(2,1)S(1)} %get-tuple-element.20), channel_id=1, source_target_pairs={{4,0},{8,4},{12,8},{16,12},{20,16},{24,20},{28,24},{5,1},{9,5},{13... | collective-permute-start | bytes 290312 | tf_op jit(solution)/shard_map/ppermute | solution.py:16
  30.5 0.7 copy-start.5
  31.2 1.8 %copy-start.6 = (bf16[6,1,1,7,6,192]{5,1,4,3,2,0:T(2,128)(2,1)}, bf16[6,1,1,7,6,192]{5,1,4,3,2,0:T(2,128)(2,1)S(1)}, u32[]{:S(2)}) copy-start(bf16[6,1,1,7,6,192]{5,1,4,3,2,0:T(2,128)(2,1)S(1)} %collective-permute-done.3) | copy-start | bytes 290308
  33.0 13.1 %collective-permute-start.4 = (bf16[6,4,1,7,6,192]{5,1,4,3,2,0:T(4,128)(2,1)}, bf16[6,4,1,7,6,192]{5,1,4,3,2,0:T(4,128)(2,1)}, u32[]{:S(2)}, u32[]{:S(2)}) collective-permute-start(bf16[6,4,1,7,6,192]{5,1,4,3,2,0:T(4,128)(2,1)} %pad_maximum_fusion.2), channel_id=1, source_target_pairs={{0,1},{1,2},{2,3},{4,5},{5,6},{6,7},{8,9},{9,10},{10,11},{12,13},{... | collective-permute-start | bytes 1161224 | tf_op jit(solution)/shard_map/ppermute | solution.py:13
  35.1 15.4 %collective-permute-start.5 = (bf16[6,4,1,7,6,192]{5,1,4,3,2,0:T(4,128)(2,1)}, bf16[6,4,1,7,6,192]{5,1,4,3,2,0:T(4,128)(2,1)}, u32[]{:S(2)}, u32[]{:S(2)}) collective-permute-start(bf16[6,4,1,7,6,192]{5,1,4,3,2,0:T(4,128)(2,1)} %pad_maximum_fusion.2), channel_id=1, source_target_pairs={{1,0},{2,1},{3,2},{5,4},{6,5},{7,6},{9,8},{10,9},{11,10},{13,12},{... | collective-permute-start | bytes 1161224 | tf_op jit(solution)/shard_map/ppermute | solution.py:16
  38.4 0.7 copy-start.2
  39.0 5.6 %copy-start.10 = (s32[8,4]{1,0:T(8,128)S(1)}, s32[8,4]{1,0:T(8,128)}, u32[]{:S(2)}) copy-start(s32[8,4]{1,0:T(8,128)} %fusion.27) | copy-start | bytes 388
  77.4 10.5 %collective-permute-start.6 = (f32[1,4,3,2268]{3,2,1,0:T(4,128)}, f32[1,4,3,2268]{3,2,1,0:T(4,128)}, u32[]{:S(2)}, u32[]{:S(2)}) collective-permute-start(f32[1,4,3,2268]{3,2,1,0:T(4,128)} %slice.136), channel_id=1, source_target_pairs={{0,32},{32,64},{64,96},{96,128},{128,160},{160,192},{192,224},{224... | collective-permute-start | bytes 326600 | tf_op jit(solution)/shard_map/ppermute | solution.py:13
  86.6 6.1 %collective-permute-start.7 = (f32[1,4,3,2268]{3,2,1,0:T(4,128)}, f32[1,4,3,2268]{3,2,1,0:T(4,128)S(1)}, u32[]{:S(2)}, u32[]{:S(2)}) collective-permute-start(f32[1,4,3,2268]{3,2,1,0:T(4,128)} %slice.138), channel_id=1, source_target_pairs={{32,0},{64,32},{96,64},{128,96},{160,128},{192,160},{224,192},{256... | collective-permute-start | bytes 326600 | tf_op jit(solution)/shard_map/ppermute | solution.py:16
  92.7 15.4 %copy-start.8 = (s32[1,8,1,8,1]{3,4,2,1,0:T(1,128)S(1)}, s32[1,8,1,8,1]{3,4,2,1,0:T(1,128)}, u32[]{:S(2)}) copy-start(s32[1,8,1,8,1]{3,4,2,1,0:T(1,128)} %param.16) | copy-start | bytes 772
  92.9 6.5 %collective-permute-start.8 = (f32[8,1,3,2268]{3,2,1,0:T(4,128)S(1)}, f32[8,1,3,2268]{3,2,1,0:T(4,128)S(1)}, u32[]{:S(2)}, u32[]{:S(2)}) collective-permute-start(f32[8,1,3,2268]{3,2,1,0:T(4,128)S(1)} %get-tuple-element.17), channel_id=1, source_target_pairs={{0,4},{4,8},{8,12},{12,16},{16,20},{20,24},{24,28},{1,5},{5,9},{9,... | collective-permute-start | bytes 653192 | tf_op jit(solution)/shard_map/ppermute | solution.py:13
  95.7 8.0 %collective-permute-start.9 = (f32[8,1,3,2268]{3,2,1,0:T(4,128)S(1)}, f32[8,1,3,2268]{3,2,1,0:T(4,128)S(1)}, u32[]{:S(2)}, u32[]{:S(2)}) collective-permute-start(f32[8,1,3,2268]{3,2,1,0:T(4,128)S(1)} %get-tuple-element.18), channel_id=1, source_target_pairs={{4,0},{8,4},{12,8},{16,12},{20,16},{24,20},{28,24},{5,1},{9,5},{13... | collective-permute-start | bytes 653192 | tf_op jit(solution)/shard_map/ppermute | solution.py:16
  104.5 8.2 %collective-permute-start.10 = (f32[8,6,1,2268]{3,2,1,0:T(1,128)S(1)}, f32[8,6,1,2268]{3,2,1,0:T(1,128)S(1)}, u32[]{:S(2)}, u32[]{:S(2)}) collective-permute-start(f32[8,6,1,2268]{3,2,1,0:T(1,128)S(1)} %get-tuple-element.15), channel_id=1, source_target_pairs={{0,1},{1,2},{2,3},{4,5},{5,6},{6,7},{8,9},{9,10},{10,11},{12,13},{... | collective-permute-start | bytes 1306376 | tf_op jit(solution)/shard_map/ppermute | solution.py:13
  106.8 10.0 %collective-permute-start.11 = (f32[8,6,1,2268]{3,2,1,0:T(1,128)S(1)}, f32[8,6,1,2268]{3,2,1,0:T(1,128)S(1)}, u32[]{:S(2)}, u32[]{:S(2)}) collective-permute-start(f32[8,6,1,2268]{3,2,1,0:T(1,128)S(1)} %get-tuple-element.16), channel_id=1, source_target_pairs={{1,0},{2,1},{3,2},{5,4},{6,5},{7,6},{9,8},{10,9},{11,10},{13,12},{... | collective-permute-start | bytes 1306376 | tf_op jit(solution)/shard_map/ppermute | solution.py:16
where the time goes:
time: 138 us; the launch traced here: 135 us
  starting transfers between devices  39.4 us (29%)
  local copies, waits for them, and re-layouts  34.1 us (25%)
  waiting for transfers between devices  20.9 us (15%)
  other arithmetic  19.7 us (14%)
  blocking collectives  15.3 us (11%)
  matrix products  5.49 us (4%)
    ppermute x6, starting transfers between devices, padded_2(): lax.ppermute(lax.slice_in_dim(block, block.shape[dim] - width, None, axis...  21.3 us
    ppermute x6, starting transfers between devices, padded_2(): lax.ppermute(lax.slice_in_dim(block, 0, width, axis=dim), axis, backward)  18.1 us
    ppermute x6, waiting for transfers between devices, padded_2(): lax.ppermute(lax.slice_in_dim(block, 0, width, axis=dim), axis, backward)  15.8 us
    all_gather x1, blocking collectives, local(): pencil = lax.all_gather(coarse_rows[None], 'gy', axis=0, tiled=True)  15.3 us
    scatter-add x1, other arithmetic, local(): jax.ops.segment_sum(term_rows, segment_ids.reshape(-1), num_segments=ext_...  7.93 us
    unnamed x34, local copies, waits for them, and re-layouts  5.77 us
    concatenate x3, other arithmetic, padded_2(): block = jnp.concatenate([low, block, high], axis=dim)  5.76 us
    gather x2, local copies, waits for them, and re-layouts, local(): jnp.asarray(box_lookup(3))  5.55 us
  transfers between devices with their start and end apart: 12, of which 7 were waited for; matrix products, arithmetic and copies ran while one was open for 16% of the time, Pallas kernels for 0%

commit v1 on v0

v1 whole, which is shorter than its diff:
```python
import functools

import jax
import jax.numpy as jnp
import numpy as np
from jax import lax
from jax.experimental import pallas as pl
from jax.experimental.pallas import tpu as pltpu
from jax.sharding import PartitionSpec as P

MESH = pl.DeviceIdType.MESH
F32 = jnp.float32
BF16 = jnp.bfloat16
AX, AY = 4, 2
NA = AX * AY
SLOTS = 4
MODES = 6
ROWS = 192
CAP = 2
WIDTH = 63 * 36
PART = 21 * 36


def points(radius):
    span = range(-radius, radius + 1)
    return [
        (x, y, z) for x in span for y in span for z in span if abs(x) + abs(y) + abs(z) <= radius
    ]


FACES, NEAR, BALL = points(1), points(2), points(3)
SELF = FACES.index((0, 0, 0))


def tables():
    table = np.full((8, 768), -1.0, np.float32)
    for e, step in enumerate(FACES):
        for d, other in enumerate(FACES):
            j = NEAR.index(tuple(p + q for p, q in zip(step, other)))
            for c in range(MODES):
                table[e, j * MODES + c] = d * 8 + c
        for j, near in enumerate(NEAR):
            o = BALL.index(tuple(p - q for p, q in zip(near, step)))
            for c in range(MODES):
                table[e, 256 + (o // 21) * 128 + (o % 21) * MODES + c] = j * MODES + c
    for a in range(MODES):
        for o in range(21):
            for c in range(MODES):
                table[7, o * 36 + a * MODES + c] = a * 128 + o * MODES + c
    return np.repeat(table[:, None], 8, axis=1)


def split(x):
    high = x.astype(BF16)
    return high, (x - high.astype(F32)).astype(BF16)


def dot(a, b):
    return jnp.dot(a, b, preferred_element_type=F32)


def dot_t(a, b):
    return lax.dot_general(a, b, (((1,), (1,)), ((), ())), preferred_element_type=F32)


def halo_place(n, e):
    x, y = n // AY, n % AY
    step = FACES[e]
    if step == (0, 0, 0):
        return n
    if step[0]:
        near = x + step[0]
        if 0 <= near < AX:
            return near * AY + y
        return (8 if step[0] < 0 else 10) + y
    if step[1]:
        near = y + step[1]
        if 0 <= near < AY:
            return x * AY + near
        return (12 if step[1] < 0 else 16) + 2 * (x % 2) + x // 2
    return (20 if step[2] < 0 else 28) + n


def kernel(
    sizes,
    p_ref, scols, pcols, nodes, owners, tables_ref, s_hbm,
    out,
    s_buf, place, order, ps, pm, wb, tbuf, tsx, tsy, tsz, xs, rows, sbuf,
    s_sem, ph_s, ph_r, t_s, t_r, o_s, o_r, own_sem,
):
    n_gx, n_gy, n_gz = sizes
    gx, gy, gz = lax.axis_index("gx"), lax.axis_index("gy"), lax.axis_index("gz")
    whole_y, whole_z = AY * n_gy, n_gz
    axes = (("gx", gx, n_gx), ("gy", gy, n_gy), ("gz", gz, n_gz))

    def beside(d):
        axis, step = next((i, s) for i, s in enumerate(FACES[d]) if s)
        name, at, count = axes[axis]
        return {name: lax.rem(at + step + count, count)}

    barrier = pltpu.get_barrier_semaphore()
    others = [{"gy": lax.rem(gy + r, n_gy)} for r in range(1, n_gy)]
    peers = [beside(d) for d in (0, 6, 2, 4)] + others
    for peer in peers:
        pl.semaphore_signal(barrier, inc=1, device_id=peer, device_id_type=MESH)

    s_copies = []
    for n in range(NA):
        copy = pltpu.make_async_copy(
            s_hbm.at[pl.ds(n * SLOTS, SLOTS)], s_buf.at[pl.ds(n * SLOTS, SLOTS)], s_sem.at[n]
        )
        copy.start()
        s_copies.append(copy)

    def direction(delta):
        found = jnp.int32(SELF)
        for size in (1, whole_z, whole_y * whole_z):
            found = found + (delta >= size).astype(jnp.int32) - (delta <= -size).astype(jnp.int32)
        return found

    p_dir, s_dir = [], []
    for n in range(NA):
        x, y = n // AY, n % AY
        own = ((gx * AX + x) * whole_y + gy * AY + y) * whole_z + gz
        p_dir.append([direction(pcols[x, y, 0, t] - own) for t in range(SLOTS)])
        s_dir.append([direction(scols[x, y, 0, t] - own) for t in range(SLOTS)])

    row32 = lax.broadcasted_iota(jnp.int32, (32, 64), 0)
    lane192 = lax.broadcasted_iota(jnp.int32, (4, ROWS), 1)
    for n in range(NA):
        x, y = n // AY, n % AY
        live = lane192 < 3 * nodes[y, 0, x]
        for c in range(MODES):
            block = p_ref[n, c].astype(F32)
            block = jnp.where(live, block, 0.0)
            ps[0, pl.ds(n * 32 + 4 * c, 4), :] = block[:, :128]
            ps[1, pl.ds(n * 32 + 4 * c, 4), pl.ds(0, 64)] = block[:, 128:]
        ps[0, pl.ds(n * 32 + 24, 8), :] = jnp.zeros((8, 128), F32)
        ps[1, pl.ds(n * 32 + 24, 8), pl.ds(0, 64)] = jnp.zeros((8, 64), F32)
        code = jnp.full((32, 64), p_dir[n][0], jnp.int32)
        for t in range(1, SLOTS):
            code = jnp.where((row32 & 3) == t, p_dir[n][t], code)
        code = jnp.where(row32 < 24, code * 8 + (row32 >> 2), -2)
        ps[1, pl.ds(n * 32, 32), pl.ds(64, 64)] = code.astype(F32)
        for k in range(2):
            pm[x, y, :, pl.ds(k * 128, 128)] = ps[k, pl.ds(n * 32, 32), :].astype(BF16)

    pl.semaphore_wait(barrier, len(peers))

    def halo(i, src, dst, d):
        copy = pltpu.make_async_remote_copy(
            src_ref=src, dst_ref=dst, send_sem=ph_s.at[i], recv_sem=ph_r.at[i],
            device_id=beside(d), device_id_type=MESH,
        )
        copy.start()
        return copy

    halos = [
        halo(0, pm.at[pl.ds(0, 4)], pm.at[pl.ds(14, 4)], 2),
        halo(1, pm.at[pl.ds(0, 4)], pm.at[pl.ds(10, 4)], 4),
        halo(2, pm.at[pl.ds(0, 2), 0], pm.at[pl.ds(8, 2), 0], 1),
        halo(3, pm.at[pl.ds(2, 2), 0], pm.at[pl.ds(8, 2), 1], 1),
        halo(4, pm.at[pl.ds(0, 2), 1], pm.at[pl.ds(6, 2), 0], 5),
        halo(5, pm.at[pl.ds(2, 2), 1], pm.at[pl.ds(6, 2), 1], 5),
        halo(6, pm.at[0], pm.at[5], 0),
        halo(7, pm.at[3], pm.at[4], 6),
    ]

    def one_hot(source, count):
        wide = source.shape[1]
        at = lax.broadcasted_iota(jnp.int32, (count, wide), 0).astype(F32)
        return jnp.where(at == jnp.concatenate([source] * (count // 8), axis=0), 1.0, 0.0).astype(BF16)

    for d in range(7):
        place[d] = one_hot(tables_ref[d, :, pl.ds(256, 384)], 256)
    order[...] = one_hot(tables_ref[7], MODES * 128)

    for n in range(NA):
        halves = []
        for k in range(2):
            parts = [ps[k, pl.ds(n * 32 + t, 8, stride=4), :] for t in range(SLOTS)]
            dense = []
            for d in range(7):
                total = jnp.zeros((8, 128), F32)
                for t in range(SLOTS):
                    mark = jnp.full((8, 128), p_dir[n][t], jnp.int32) == d
                    total = jnp.where(mark, parts[t], total)
                dense.append(total)
            dense.append(jnp.zeros((8, 128), F32))
            halves.append(jnp.concatenate(dense, axis=0))
        dense = jnp.concatenate([halves[0], halves[1][:, :64]], axis=1).astype(BF16)
        s_copies[n].wait()
        for s in range(SLOTS):
            high, low = split(dot(dense, s_buf[n * SLOTS + s]))
            wb[n, pl.ds(s * 128, 64), :] = high
            wb[n, pl.ds(s * 128 + 64, 64), :] = low

    for copy in halos:
        copy.wait()

    lane128 = lax.broadcasted_iota(jnp.int32, (128, 128), 1) // 32

    def term(i, src, dst, d):
        copy = pltpu.make_async_remote_copy(
            src_ref=src, dst_ref=dst, send_sem=t_s.at[i], recv_sem=t_r.at[i],
            device_id=beside(d), device_id_type=MESH,
        )
        copy.start()
        return copy

    terms = {}
    for n in range(NA):
        x, y = n // AY, n % AY
        tables, picks = [], []
        for s in range(SLOTS):
            e = s_dir[n][s]
            at = jnp.int32(halo_place(n, 0))
            for other in range(1, 7):
                at = jnp.where(e == other, halo_place(n, other), at)
            table = pm[at // AY, at % AY]
            tables.append(table[:, :ROWS])
            code = jnp.broadcast_to(table[:, ROWS:ROWS + 1].astype(F32), (32, 256))
            wanted = tables_ref[e, :, pl.ds(0, 256)]
            wanted = jnp.concatenate([wanted] * 4, axis=0)
            picks.append(jnp.where(code == wanted, 1.0, 0.0).astype(BF16))
        full = dot_t(wb[n], jnp.concatenate(tables, axis=0))
        z = jnp.zeros((128, 128), F32)
        for s in range(SLOTS):
            z = jnp.where(lane128 == s, full[s * 128:(s + 1) * 128], z)
        high, low = split(z[:64] + z[64:])
        both = dot(jnp.concatenate([high, low], axis=0), jnp.concatenate(picks, axis=0))
        t_all = both[:64] + both[64:]
        for d, step in enumerate(FACES):
            block = t_all[d * 8:d * 8 + 8]
            to_x, to_y = x + step[0], y + step[1]
            if step[2]:
                tsz[0 if step[2] < 0 else 1, x, y] = block
            elif not 0 <= to_x < AX:
                tsx[0 if step[0] < 0 else 1, y] = block
            elif not 0 <= to_y < AY:
                tsy[0 if step[1] < 0 else 1, x] = block
            else:
                tbuf[d, to_x, to_y] = block
        if n == 1:
            terms[0] = term(0, tsx.at[0], tbuf.at[0, 3], 0)
        if n == NA - 1:
            terms[2] = term(1, tsz.at[0], tbuf.at[2], 2)
            terms[4] = term(2, tsz.at[1], tbuf.at[4], 4)
            terms[1] = term(3, tsy.at[0], tbuf.at[1, :, 1], 1)
            terms[5] = term(4, tsy.at[1], tbuf.at[5, :, 0], 5)
            terms[6] = term(5, tsx.at[1], tbuf.at[6, 0], 6)

    total = jnp.zeros((128, 384), F32)
    for d in (3, 0, 6, 1, 5, 2, 4):
        if d in terms:
            terms[d].wait()
        high, low = split(tbuf[d].reshape(64, 256))
        total = total + dot(jnp.concatenate([high, low], axis=0), place[d])
    total = total[:64] + total[64:]
    for v in range(3):
        xs[v] = total[:, v * 128:v * 128 + 128]

    stacked = []
    for v in range(3):
        stacked.append(
            jnp.concatenate(
                [xs[v, pl.ds(a, 8, stride=8), :] for a in range(MODES)], axis=1
            )
        )
    high, low = split(jnp.concatenate(stacked, axis=0))
    flat = dot(jnp.concatenate([high, low], axis=0), order[...])
    flat = flat[:24] + flat[24:]
    for v in range(3):
        rows[:, pl.ds(v * PART, PART)] = flat[v * 8:v * 8 + 8, :PART]

    owner = [owners[0, gy, 0, 0, q] for q in range(NA)]
    spot = []
    for q in range(NA):
        rank = jnp.int32(0)
        for other in range(q):
            rank = rank + (owner[other] == owner[q]).astype(jnp.int32)
        spot.append(owner[q] * CAP + rank)
    row2 = lax.broadcasted_iota(jnp.int32, (CAP, WIDTH), 0)
    for target in range(n_gy):
        chosen = jnp.zeros((CAP, WIDTH), F32)
        for q in range(NA):
            row = jnp.broadcast_to(rows[pl.ds(q, 1), pl.ds(0, WIDTH)], (CAP, WIDTH))
            chosen = jnp.where(row2 + target * CAP == spot[q], row, chosen)
        sbuf[target] = chosen
    sends = []
    for r in range(1, n_gy):
        target = lax.rem(gy + r, n_gy)
        copy = pltpu.make_async_remote_copy(
            src_ref=sbuf.at[target], dst_ref=out.at[gy], send_sem=o_s.at[r - 1], recv_sem=o_r.at[r - 1],
            device_id={"gy": target}, device_id_type=MESH,
        )
        copy.start()
        sends.append(copy)
    mine = pltpu.make_async_copy(sbuf.at[gy], out.at[gy], own_sem)
    mine.start()
    for copy in sends:
        copy.wait()
    mine.wait()


def local(sizes, stiff_blocks, stiff_cols, prolong_blocks, prolong_cols, agg_nodes, row_owner):
    n_gy = sizes[1]
    smem = pl.BlockSpec(memory_space=pltpu.SMEM)
    vmem = pl.BlockSpec(memory_space=pltpu.VMEM)
    hbm = pl.BlockSpec(memory_space=pltpu.HBM)
    out = pl.pallas_call(
        functools.partial(kernel, sizes),
        out_shape=jax.ShapeDtypeStruct((n_gy, CAP, WIDTH), F32),
        in_specs=[vmem, smem, smem, smem, smem, vmem, hbm],
        out_specs=hbm,
        scratch_shapes=[
            pltpu.VMEM((NA * SLOTS, ROWS, ROWS), BF16),
            pltpu.VMEM((7, 256, 384), BF16),
            pltpu.VMEM((MODES * 128, MODES * 128), BF16),
            pltpu.VMEM((2, NA * 32, 128), F32),
            pltpu.VMEM((18, AY, 32, 256), BF16),
            pltpu.VMEM((NA, 512, ROWS), BF16),
            pltpu.VMEM((7, AX, AY, 8, 256), F32),
            pltpu.VMEM((2, AY, 8, 256), F32),
            pltpu.VMEM((2, AX, 8, 256), F32),
            pltpu.VMEM((2, AX, AY, 8, 256), F32),
            pltpu.VMEM((3, 64, 128), F32),
            pltpu.VMEM((8, 2304), F32),
            pltpu.VMEM((n_gy, CAP, WIDTH), F32),
            pltpu.SemaphoreType.DMA((NA,)),
            pltpu.SemaphoreType.DMA((8,)),
            pltpu.SemaphoreType.DMA((8,)),
            pltpu.SemaphoreType.DMA((6,)),
            pltpu.SemaphoreType.DMA((6,)),
            pltpu.SemaphoreType.DMA((n_gy - 1,)),
            pltpu.SemaphoreType.DMA((n_gy - 1,)),
            pltpu.SemaphoreType.DMA,
        ],
        compiler_params=pltpu.CompilerParams(
            collective_id=0, has_side_effects=True, vmem_limit_bytes=40 * 1024 * 1024
        ),
        name="galerkin",
    )(
        prolong_blocks.transpose(0, 1, 2, 4, 3, 5).reshape(NA, MODES, SLOTS, ROWS),
        stiff_cols,
        prolong_cols,
        agg_nodes.transpose(1, 2, 0),
        row_owner.transpose(0, 1, 2, 4, 3),
        jnp.asarray(tables()),
        stiff_blocks.reshape(NA * SLOTS, ROWS, ROWS),
    )
    return out[None, :, None]


def solution(mesh):
    sizes = (mesh.shape["gx"], mesh.shape["gy"], mesh.shape["gz"])
    return jax.shard_map(
        functools.partial(local, sizes),
        mesh=mesh,
        in_specs=(
            P("gx", "gy", "gz", None, None, None),
            P("gx", "gy", "gz", None),
            P("gx", "gy", "gz", None, None, None),
            P("gx", "gy", "gz", None),
            P("gx", "gy", "gz"),
            P("gx", None, "gz", None, None),
        ),
        out_specs=P("gx", "gy", "gz", None, None),
        check_vma=False,
    )
```

time: 138 us -> 46.7 us (0.34); the launches traced: 135 us -> 46.3 us
  starting transfers between devices: 39.4 us -> 0 us
  Pallas kernels: 0 us -> 39.2 us
  local copies, waits for them, and re-layouts: 34.1 us -> 7.11 us
  waiting for transfers between devices: 20.9 us -> 0 us
  other arithmetic: 19.7 us -> 0 us
  blocking collectives: 15.3 us -> 0 us
  matrix products: 5.49 us -> 0 us
    ppermute x12 -> x0, starting transfers between devices: 39.4 us -> none  [the longest x6 21.3 us: padded_2(): lax.ppermute(lax.slice_in_dim(block, block.shape[dim] - width, None, axis...]
    pallas_call x0 -> x1, Pallas kernels: none -> 39.2 us  [local(): pl.pallas_call(functools.partial(kernel, sizes), out_shape=jax.ShapeDtype...]
    ppermute x12 -> x0, waiting for transfers between devices: 20.9 us -> none  [the longest x6 15.8 us: padded_2(): lax.ppermute(lax.slice_in_dim(block, 0, width, axis=dim), axis, backward)]
    all_gather x1 -> x0, blocking collectives: 15.3 us -> none  [local(): pencil = lax.all_gather(coarse_rows[None], 'gy', axis=0, tiled=True)]
    gather x7 -> x0, local copies, waits for them, and re-layouts: 11.3 us -> none  [the longest x2 5.55 us: local(): jnp.asarray(box_lookup(3))]
    scatter-add x1 -> x0, other arithmetic: 7.93 us -> none  [local(): jax.ops.segment_sum(term_rows, segment_ids.reshape(-1), num_segments=ext_...]
    reshape x3 -> x0, local copies, waits for them, and re-layouts: 6.02 us -> none  [the longest x1 3.47 us: local(): partial_value.reshape(block_x + 2, ext_y, ext_z, ball_count * mode_square)]
    slice x6 -> x0, local copies, waits for them, and re-layouts: 5.8 us -> none  [the longest x3 3.44 us: padded_2(): lax.slice_in_dim(block, 0, width, axis=dim)]
  transfers between devices with their start and end apart: 12 -> 0, of which waited for: 7 -> 0; matrix products, arithmetic and copies ran while one was open for 16% -> 0% of each run, Pallas kernels for 0% -> 0%
where the time goes in v1:
time: 46.7 us; the launch traced here: 46.3 us
  Pallas kernels  39.2 us (84%)
  local copies, waits for them, and re-layouts  7.11 us (15%)
    pallas_call x1, Pallas kernels, local(): pl.pallas_call(functools.partial(kernel, sizes), out_shape=jax.ShapeDtype...  39.2 us
    unnamed x15, local copies, waits for them, and re-layouts  7.11 us

profile of v1, /device:TPU:1, one launch (start us, length us, event | category | flops | bytes accessed | tf_op | source)
XLA Modules:
  0.0 46.3 jit_solution(253880320414833016)
XLA Ops:
  0.0 0.0 copy-start
  0.0 1.9 %copy-done = bf16[4,2,1,4,192,192]{5,4,3,2,1,0:T(8,128)(2,1)S(1)} copy-done((bf16[4,2,1,4,192,192]{5,4,3,2,1,0:T(8,128)(2,1)S(1)}, bf16[4,2,1,4,192,192]{5,4,3,2,1,0:T(8,128)(2,1)}, u32[]{:S(2)}) %copy-start) | copy-done | bytes 2359320
  1.9 0.0 copy-start.1
  1.9 0.9 %copy-done.1 = f32[8,8,768]{2,1,0:T(8,128)S(1)} copy-done((f32[8,8,768]{2,1,0:T(8,128)S(1)}, f32[8,8,768]{2,1,0:T(8,128)}, u32[]{:S(2)}) %copy-start.1) | copy-done | bytes 196632
  2.8 0.0 copy-start.2
  2.8 0.9 %copy-done.2 = bf16[4,2,1,4,6,192]{5,3,4,2,1,0:T(4,128)(2,1)S(1)} copy-done((bf16[4,2,1,4,6,192]{5,3,4,2,1,0:T(4,128)(2,1)S(1)}, bf16[4,2,1,4,6,192]{5,3,4,2,1,0:T(4,128)(2,1)}, u32[]{:S(2)}) %copy-start.2) | copy-done | bytes 73752
  3.7 0.0 copy-start.3
  3.7 0.7 %copy-done.3 = s32[4,2,1,4]{3,2,1,0:T(1,128)S(1)} copy-done((s32[4,2,1,4]{3,2,1,0:T(1,128)S(1)}, s32[4,2,1,4]{3,2,1,0:T(1,128)}, u32[]{:S(2)}) %copy-start.3) | copy-done | bytes 152
  4.4 0.0 copy-start.4
  4.4 0.7 %copy-done.4 = s32[4,2,1,4]{3,2,1,0:T(1,128)S(1)} copy-done((s32[4,2,1,4]{3,2,1,0:T(1,128)S(1)}, s32[4,2,1,4]{3,2,1,0:T(1,128)}, u32[]{:S(2)}) %copy-start.4) | copy-done | bytes 152
  5.1 0.0 copy-start.5
  5.1 0.7 %copy-done.5 = s32[1,8,1,8,1]{3,4,2,1,0:T(1,128)S(1)} copy-done((s32[1,8,1,8,1]{3,4,2,1,0:T(1,128)S(1)}, s32[1,8,1,8,1]{3,4,2,1,0:T(1,128)}, u32[]{:S(2)}) %copy-start.5) | copy-done | bytes 280
  5.8 0.0 copy-start.6
  5.8 0.7 %copy-done.6 = s32[4,2,1]{0,2,1:T(1,128)S(1)} copy-done((s32[4,2,1]{0,2,1:T(1,128)S(1)}, s32[4,2,1]{0,2,1:T(1,128)}, u32[]{:S(2)}) %copy-start.6) | copy-done | bytes 56
  6.5 39.2 %galerkin.1 = f32[8,2,2268]{2,1,0:T(2,128)S(1)} custom-call(bf16[8,6,4,192]{3,2,1,0:T(4,128)(2,1)S(1)} %bitcast.13, s32[4,2,1,4]{3,2,1,0:T(1,128)S(1)} %copy-done.3, s32[4,2,1,4]{3,2,1,0:T(1,128)S(1)} %copy-done.4, s32[2,1,4]{2,1,0:T(1,128)S(1)} %bitcast.15, s32[1,8,1,1,8]{4,3,2,1,0:T(1,128)S(1)} %bitcast.14, f32[8,8,768]{2,1,0:T(8,128)S(1)} %copy-done.1, ...), custom_call_target="tpu_custom_call" | custom-call | tf_op jit(solution)/shard_map/galerkin/pallas_call | solution.py:311
  45.7 0.7 %copy.11 = f32[1,8,1,2,2268]{4,3,2,1,0:T(2,128)} copy(f32[1,8,1,2,2268]{4,3,2,1,0:T(2,128)S(1)} %bitcast.12) | data formatting | bytes 290304
Async XLA Ops:
  0.0 1.9 %copy-start = (bf16[4,2,1,4,192,192]{5,4,3,2,1,0:T(8,128)(2,1)S(1)}, bf16[4,2,1,4,192,192]{5,4,3,2,1,0:T(8,128)(2,1)}, u32[]{:S(2)}) copy-start(bf16[4,2,1,4,192,192]{5,4,3,2,1,0:T(8,128)(2,1)} %param.7) | copy-start | bytes 7077892
  1.9 0.9 %copy-start.1 = (f32[8,8,768]{2,1,0:T(8,128)S(1)}, f32[8,8,768]{2,1,0:T(8,128)}, u32[]{:S(2)}) copy-start(f32[8,8,768]{2,1,0:T(8,128)} %constant.2.clone.tables_ref) | copy-start | bytes 589828
  2.8 0.9 %copy-start.2 = (bf16[4,2,1,4,6,192]{5,3,4,2,1,0:T(4,128)(2,1)S(1)}, bf16[4,2,1,4,6,192]{5,3,4,2,1,0:T(4,128)(2,1)}, u32[]{:S(2)}) copy-start(bf16[4,2,1,4,6,192]{5,3,4,2,1,0:T(4,128)(2,1)} %param.9) | copy-start | bytes 221188
  3.7 0.7 %copy-start.3 = (s32[4,2,1,4]{3,2,1,0:T(1,128)S(1)}, s32[4,2,1,4]{3,2,1,0:T(1,128)}, u32[]{:S(2)}) copy-start(s32[4,2,1,4]{3,2,1,0:T(1,128)} %scols.1) | copy-start | bytes 388
  4.4 0.7 %copy-start.4 = (s32[4,2,1,4]{3,2,1,0:T(1,128)S(1)}, s32[4,2,1,4]{3,2,1,0:T(1,128)}, u32[]{:S(2)}) copy-start(s32[4,2,1,4]{3,2,1,0:T(1,128)} %pcols.1) | copy-start | bytes 388
  5.1 0.7 %copy-start.5 = (s32[1,8,1,8,1]{3,4,2,1,0:T(1,128)S(1)}, s32[1,8,1,8,1]{3,4,2,1,0:T(1,128)}, u32[]{:S(2)}) copy-start(s32[1,8,1,8,1]{3,4,2,1,0:T(1,128)} %param.12) | copy-start | bytes 772
  5.8 0.7 %copy-start.6 = (s32[4,2,1]{0,2,1:T(1,128)S(1)}, s32[4,2,1]{0,2,1:T(1,128)}, u32[]{:S(2)}) copy-start(s32[4,2,1]{0,2,1:T(1,128)} %param.11) | copy-start | bytes 100

commit v2 on v1

--- a/solution.py
+++ b/solution.py
@@ -83,27 +83,37 @@
 
 def kernel(
     sizes,
-    p_ref, scols, pcols, nodes, owners, tables_ref, s_hbm,
+    p_hbm, scols_hbm, pcols_hbm, nodes_hbm, owners_hbm, tables_hbm, s_hbm,
     out,
+    p_ref, scols, pcols, nodes, owners, tables_ref,
     s_buf, place, order, ps, pm, wb, tbuf, tsx, tsy, tsz, xs, rows, sbuf,
-    s_sem, ph_s, ph_r, t_s, t_r, o_s, o_r, own_sem,
+    in_sem, s_sem, ph_s, ph_r, t_s, t_r, o_s, o_r, own_sem,
 ):
     n_gx, n_gy, n_gz = sizes
     gx, gy, gz = lax.axis_index("gx"), lax.axis_index("gy"), lax.axis_index("gz")
     whole_y, whole_z = AY * n_gy, n_gz
     axes = (("gx", gx, n_gx), ("gy", gy, n_gy), ("gz", gz, n_gz))
 
+    def axis_of(d):
+        return next((axes[i] + (step,) for i, step in enumerate(FACES[d]) if step))
+
     def beside(d):
-        axis, step = next((i, s) for i, s in enumerate(FACES[d]) if s)
-        name, at, count = axes[axis]
-        return {name: lax.rem(at + step + count, count)}
-
-    barrier = pltpu.get_barrier_semaphore()
-    others = [{"gy": lax.rem(gy + r, n_gy)} for r in range(1, n_gy)]
-    peers = [beside(d) for d in (0, 6, 2, 4)] + others
-    for peer in peers:
-        pl.semaphore_signal(barrier, inc=1, device_id=peer, device_id_type=MESH)
-
+        name, at, count, step = axis_of(d)
+        return {name: at + step}
+
+    def exists(d):
+        name, at, count, step = axis_of(d)
+        return at > 0 if step < 0 else at < count - 1
+
+    loads = [
+        pltpu.make_async_copy(src, dst, in_sem.at[i])
+        for i, (src, dst) in enumerate([
+            (pcols_hbm, pcols), (nodes_hbm, nodes), (p_hbm, p_ref),
+            (scols_hbm, scols), (owners_hbm, owners), (tables_hbm, tables_ref),
+        ])
+    ]
+    for copy in loads:
+        copy.start()
     s_copies = []
     for n in range(NA):
         copy = pltpu.make_async_copy(
@@ -112,18 +122,35 @@
         copy.start()
         s_copies.append(copy)
 
+    barrier = pltpu.get_barrier_semaphore()
+    others = [{"gy": lax.rem(gy + r, n_gy)} for r in range(1, n_gy)]
+    greeted = jnp.int32(len(others))
+    for peer in others:
+        pl.semaphore_signal(barrier, inc=1, device_id=peer, device_id_type=MESH)
+    for d in (0, 6, 2, 4):
+        greeted = greeted + exists(d).astype(jnp.int32)
+
+        @pl.when(exists(d))
+        def _():
+            pl.semaphore_signal(barrier, inc=1, device_id=beside(d), device_id_type=MESH)
+
+    for copy in loads[:3]:
+        copy.wait()
+
     def direction(delta):
         found = jnp.int32(SELF)
         for size in (1, whole_z, whole_y * whole_z):
             found = found + (delta >= size).astype(jnp.int32) - (delta <= -size).astype(jnp.int32)
         return found
 
-    p_dir, s_dir = [], []
+    def own_id(n):
+        return ((gx * AX + n // AY) * whole_y + gy * AY + n % AY) * whole_z + gz
+
+    p_dir = []
     for n in range(NA):
         x, y = n // AY, n % AY
-        own = ((gx * AX + x) * whole_y + gy * AY + y) * whole_z + gz
+        own = own_id(n)
         p_dir.append([direction(pcols[x, y, 0, t] - own) for t in range(SLOTS)])
-        s_dir.append([direction(scols[x, y, 0, t] - own) for t in range(SLOTS)])
 
     row32 = lax.broadcasted_iota(jnp.int32, (32, 64), 0)
     lane192 = lax.broadcasted_iota(jnp.int32, (4, ROWS), 1)
@@ -145,15 +172,36 @@
         for k in range(2):
             pm[x, y, :, pl.ds(k * 128, 128)] = ps[k, pl.ds(n * 32, 32), :].astype(BF16)
 
-    pl.semaphore_wait(barrier, len(peers))
-
-    def halo(i, src, dst, d):
+    pl.semaphore_wait(barrier, greeted)
+
+    def exchange(i, src, dst, d, send_sem, recv_sem):
         copy = pltpu.make_async_remote_copy(
-            src_ref=src, dst_ref=dst, send_sem=ph_s.at[i], recv_sem=ph_r.at[i],
+            src_ref=src, dst_ref=dst, send_sem=send_sem.at[i], recv_sem=recv_sem.at[i],
             device_id=beside(d), device_id_type=MESH,
         )
-        copy.start()
-        return copy
+
+        @pl.when(exists(d))
+        def _():
+            copy.start()
+
+        @pl.when(jnp.logical_not(exists(6 - d)))
+        def _():
+            dst[...] = jnp.zeros(dst.shape, dst.dtype)
+
+        def arrived():
+            @pl.when(exists(6 - d))
+            def _():
+                copy.wait_recv()
+
+        def sent():
+            @pl.when(exists(d))
+            def _():
+                copy.wait_send()
+
+        return arrived, sent
+
+    def halo(i, src, dst, d):
+        return exchange(i, src, dst, d, ph_s, ph_r)
 
     halos = [
         halo(0, pm.at[pl.ds(0, 4)], pm.at[pl.ds(14, 4)], 2),
@@ -165,15 +213,6 @@
         halo(6, pm.at[0], pm.at[5], 0),
         halo(7, pm.at[3], pm.at[4], 6),
     ]
-
-    def one_hot(source, count):
-        wide = source.shape[1]
-        at = lax.broadcasted_iota(jnp.int32, (count, wide), 0).astype(F32)
-        return jnp.where(at == jnp.concatenate([source] * (count // 8), axis=0), 1.0, 0.0).astype(BF16)
-
-    for d in range(7):
-        place[d] = one_hot(tables_ref[d, :, pl.ds(256, 384)], 256)
-    order[...] = one_hot(tables_ref[7], MODES * 128)
 
     for n in range(NA):
         halves = []
@@ -195,18 +234,19 @@
             wb[n, pl.ds(s * 128, 64), :] = high
             wb[n, pl.ds(s * 128 + 64, 64), :] = low
 
-    for copy in halos:
+    for copy in loads[3:]:
         copy.wait()
+    s_dir = []
+    for n in range(NA):
+        x, y = n // AY, n % AY
+        s_dir.append([direction(scols[x, y, 0, s] - own_id(n)) for s in range(SLOTS)])
+    for arrived, _ in halos:
+        arrived()
 
     lane128 = lax.broadcasted_iota(jnp.int32, (128, 128), 1) // 32
 
     def term(i, src, dst, d):
-        copy = pltpu.make_async_remote_copy(
-            src_ref=src, dst_ref=dst, send_sem=t_s.at[i], recv_sem=t_r.at[i],
-            device_id=beside(d), device_id_type=MESH,
-        )
-        copy.start()
-        return copy
+        return exchange(i, src, dst, d, t_s, t_r)
 
     terms = {}
     for n in range(NA):
@@ -250,10 +290,21 @@
             terms[5] = term(4, tsy.at[1], tbuf.at[5, :, 0], 5)
             terms[6] = term(5, tsx.at[1], tbuf.at[6, 0], 6)
 
+    def one_hot(source, base):
+        wide = source.shape[1]
+        at = lax.broadcasted_iota(jnp.int32, (128, wide), 0).astype(F32) + base
+        return jnp.where(at == jnp.concatenate([source] * 16, axis=0), 1.0, 0.0).astype(BF16)
+
+    for d in (3, 0, 6, 1, 5, 2, 4):
+        for k in range(2):
+            place[d, pl.ds(k * 128, 128), :] = one_hot(tables_ref[d, :, pl.ds(256, 384)], k * 128.0)
+    for a in range(MODES):
+        order[pl.ds(a * 128, 128), :] = one_hot(tables_ref[7], a * 128.0)
+
     total = jnp.zeros((128, 384), F32)
     for d in (3, 0, 6, 1, 5, 2, 4):
         if d in terms:
-            terms[d].wait()
+            terms[d][0]()
         high, low = split(tbuf[d].reshape(64, 256))
         total = total + dot(jnp.concatenate([high, low], axis=0), place[d])
     total = total[:64] + total[64:]
@@ -301,19 +352,25 @@
     for copy in sends:
         copy.wait()
     mine.wait()
+    for _, sent in halos + list(terms.values()):
+        sent()
 
 
 def local(sizes, stiff_blocks, stiff_cols, prolong_blocks, prolong_cols, agg_nodes, row_owner):
     n_gy = sizes[1]
-    smem = pl.BlockSpec(memory_space=pltpu.SMEM)
-    vmem = pl.BlockSpec(memory_space=pltpu.VMEM)
     hbm = pl.BlockSpec(memory_space=pltpu.HBM)
     out = pl.pallas_call(
         functools.partial(kernel, sizes),
         out_shape=jax.ShapeDtypeStruct((n_gy, CAP, WIDTH), F32),
-        in_specs=[vmem, smem, smem, smem, smem, vmem, hbm],
+        in_specs=[hbm] * 7,
         out_specs=hbm,
         scratch_shapes=[
+            pltpu.VMEM((NA, MODES, SLOTS, ROWS), BF16),
+            pltpu.SMEM(stiff_cols.shape, jnp.int32),
+            pltpu.SMEM(prolong_cols.shape, jnp.int32),
+            pltpu.SMEM((AY, 1, AX), jnp.int32),
+            pltpu.SMEM((1, n_gy, 1, 1, NA), jnp.int32),
+            pltpu.VMEM((8, 8, 768), F32),
             pltpu.VMEM((NA * SLOTS, ROWS, ROWS), BF16),
             pltpu.VMEM((7, 256, 384), BF16),
             pltpu.VMEM((MODES * 128, MODES * 128), BF16),
@@ -327,6 +384,7 @@
             pltpu.VMEM((3, 64, 128), F32),
             pltpu.VMEM((8, 2304), F32),
             pltpu.VMEM((n_gy, CAP, WIDTH), F32),
+            pltpu.SemaphoreType.DMA((6,)),
             pltpu.SemaphoreType.DMA((NA,)),
             pltpu.SemaphoreType.DMA((8,)),
             pltpu.SemaphoreType.DMA((8,)),
@@ -337,7 +395,7 @@
             pltpu.SemaphoreType.DMA,
         ],
         compiler_params=pltpu.CompilerParams(
-            collective_id=0, has_side_effects=True, vmem_limit_bytes=40 * 1024 * 1024
+            collective_id=0, has_side_effects=True, vmem_limit_bytes=62 * 1024 * 1024
         ),
         name="galerkin",
     )(

time: 46.7 us -> 34.1 us (0.73)
  Pallas kernels: 39.2 us -> 32.3 us
  local copies, waits for them, and re-layouts: 7.11 us -> 1.58 us
    pallas_call x1, Pallas kernels: 39.2 us -> 32.3 us  [local(): pl.pallas_call(functools.partial(kernel, sizes), out_shape=jax.ShapeDtype...]
    unnamed x15 -> x1, local copies, waits for them, and re-layouts: 7.11 us -> 1.58 us
where the time goes in v2:
time: 34.1 us; the launch traced here: 33.9 us
  Pallas kernels  32.3 us (95%)
  local copies, waits for them, and re-layouts  1.58 us (5%)
    pallas_call x1, Pallas kernels, local(): pl.pallas_call(functools.partial(kernel, sizes), out_shape=jax.ShapeDtype...  32.3 us
    unnamed x1, local copies, waits for them, and re-layouts  1.58 us

profile of v2, /device:TPU:1, one launch (start us, length us, event | category | flops | bytes accessed | tf_op | source)
XLA Modules:
  0.0 33.9 jit_solution(2670954882656493706)
XLA Ops:
  0.0 32.3 %galerkin.1 = f32[8,2,2268]{2,1,0:T(2,128)} custom-call(bf16[8,6,4,192]{3,2,1,0:T(4,128)(2,1)} %bitcast.13, s32[4,2,1,4]{3,2,1,0:T(1,128)} %scols_hbm.1, s32[4,2,1,4]{3,2,1,0:T(1,128)} %pcols_hbm.1, s32[2,1,4]{2,1,0:T(1,128)} %bitcast.15, s32[1,8,1,1,8]{4,3,2,1,0:T(1,128)} %bitcast.14, f32[8,8,768]{2,1,0:T(8,128)} %constant.2.clone.tables_hbm, ...), custom_call_target="tpu_custom_call" | custom-call | tf_op jit(solution)/shard_map/galerkin/pallas_call | solution.py:362
  32.4 1.6 %copy.11 = f32[1,8,1,2,2268]{4,3,2,1,0:T(2,128)} copy(f32[1,8,1,2,2268]{4,3,2,1,0:T(2,128)} %bitcast.12) | data formatting | bytes 290304

commit v3 on v2

--- a/solution.py
+++ b/solution.py
@@ -72,13 +72,13 @@
         near = x + step[0]
         if 0 <= near < AX:
             return near * AY + y
-        return (8 if step[0] < 0 else 10) + y
+        return (4 if step[0] < 0 else 5) * AY + y
     if step[1]:
         near = y + step[1]
         if 0 <= near < AY:
             return x * AY + near
-        return (12 if step[1] < 0 else 16) + 2 * (x % 2) + x // 2
-    return (20 if step[2] < 0 else 28) + n
+        return (6 + x) * AY + 1 if step[1] < 0 else (10 + x) * AY
+    return (14 if step[2] < 0 else 18) * AY + n
 
 
 def kernel(
@@ -152,7 +152,7 @@
         own = own_id(n)
         p_dir.append([direction(pcols[x, y, 0, t] - own) for t in range(SLOTS)])
 
-    row32 = lax.broadcasted_iota(jnp.int32, (32, 64), 0)
+    row24 = lax.broadcasted_iota(jnp.int32, (24, 64), 0)
     lane192 = lax.broadcasted_iota(jnp.int32, (4, ROWS), 1)
     for n in range(NA):
         x, y = n // AY, n % AY
@@ -160,21 +160,26 @@
         for c in range(MODES):
             block = p_ref[n, c].astype(F32)
             block = jnp.where(live, block, 0.0)
-            ps[0, pl.ds(n * 32 + 4 * c, 4), :] = block[:, :128]
-            ps[1, pl.ds(n * 32 + 4 * c, 4), pl.ds(0, 64)] = block[:, 128:]
-        ps[0, pl.ds(n * 32 + 24, 8), :] = jnp.zeros((8, 128), F32)
-        ps[1, pl.ds(n * 32 + 24, 8), pl.ds(0, 64)] = jnp.zeros((8, 64), F32)
-        code = jnp.full((32, 64), p_dir[n][0], jnp.int32)
+            ps[0, pl.ds(n * 24 + 4 * c, 4), :] = block[:, :128]
+            ps[1, pl.ds(n * 24 + 4 * c, 4), pl.ds(0, 64)] = block[:, 128:]
+        code = jnp.full((24, 64), p_dir[n][0], jnp.int32)
         for t in range(1, SLOTS):
-            code = jnp.where((row32 & 3) == t, p_dir[n][t], code)
-        code = jnp.where(row32 < 24, code * 8 + (row32 >> 2), -2)
-        ps[1, pl.ds(n * 32, 32), pl.ds(64, 64)] = code.astype(F32)
+            code = jnp.where((row24 & 3) == t, p_dir[n][t], code)
+        code = code * 8 + (row24 >> 2)
+        ps[1, pl.ds(n * 24, 24), pl.ds(64, 64)] = code.astype(F32)
+    for k in range(2):
+        ps[k, pl.ds(NA * 24, 8), :] = jnp.zeros((8, 128), F32)
+    for x in range(AX):
         for k in range(2):
-            pm[x, y, :, pl.ds(k * 128, 128)] = ps[k, pl.ds(n * 32, 32), :].astype(BF16)
+            first, second = [ps[k, pl.ds((x * AY + y) * 24, 24), :] for y in range(AY)]
+            lanes = pl.ds(k * 128, 128)
+            pm[x, 0, :, lanes] = first[:16].astype(BF16)
+            pm[x, 1, :, lanes] = jnp.concatenate([first[16:], second[16:]], axis=0).astype(BF16)
+            pm[x, 2, :, lanes] = second[:16].astype(BF16)
 
     pl.semaphore_wait(barrier, greeted)
 
-    def exchange(i, src, dst, d, send_sem, recv_sem):
+    def exchange(i, src, dst, d, send_sem, recv_sem, fill):
         copy = pltpu.make_async_remote_copy(
             src_ref=src, dst_ref=dst, send_sem=send_sem.at[i], recv_sem=recv_sem.at[i],
             device_id=beside(d), device_id_type=MESH,
@@ -186,7 +191,7 @@
 
         @pl.when(jnp.logical_not(exists(6 - d)))
         def _():
-            dst[...] = jnp.zeros(dst.shape, dst.dtype)
+            fill[...] = jnp.zeros(fill.shape, fill.dtype)
 
         def arrived():
             @pl.when(exists(6 - d))
@@ -201,38 +206,31 @@
         return arrived, sent
 
     def halo(i, src, dst, d):
-        return exchange(i, src, dst, d, ph_s, ph_r)
-
+        return exchange(i, src, dst, d, ph_s, ph_r, dst)
+
+    four = pl.ds(0, 4)
     halos = [
-        halo(0, pm.at[pl.ds(0, 4)], pm.at[pl.ds(14, 4)], 2),
-        halo(1, pm.at[pl.ds(0, 4)], pm.at[pl.ds(10, 4)], 4),
-        halo(2, pm.at[pl.ds(0, 2), 0], pm.at[pl.ds(8, 2), 0], 1),
-        halo(3, pm.at[pl.ds(2, 2), 0], pm.at[pl.ds(8, 2), 1], 1),
-        halo(4, pm.at[pl.ds(0, 2), 1], pm.at[pl.ds(6, 2), 0], 5),
-        halo(5, pm.at[pl.ds(2, 2), 1], pm.at[pl.ds(6, 2), 1], 5),
-        halo(6, pm.at[0], pm.at[5], 0),
-        halo(7, pm.at[3], pm.at[4], 6),
+        halo(0, pm.at[four], pm.at[pl.ds(18, 4)], 2),
+        halo(1, pm.at[four], pm.at[pl.ds(14, 4)], 4),
+        halo(2, pm.at[four, pl.ds(0, 2)], pm.at[pl.ds(10, 4), pl.ds(0, 2)], 1),
+        halo(3, pm.at[four, pl.ds(1, 2)], pm.at[pl.ds(6, 4), pl.ds(1, 2)], 5),
+        halo(4, pm.at[0], pm.at[5], 0),
+        halo(5, pm.at[3], pm.at[4], 6),
     ]
+    pm[pl.ds(10, 4), 2] = jnp.zeros((4, 16, 256), BF16)
+    pm[pl.ds(6, 4), 0] = jnp.zeros((4, 16, 256), BF16)
 
     for n in range(NA):
-        halves = []
-        for k in range(2):
-            parts = [ps[k, pl.ds(n * 32 + t, 8, stride=4), :] for t in range(SLOTS)]
-            dense = []
-            for d in range(7):
-                total = jnp.zeros((8, 128), F32)
-                for t in range(SLOTS):
-                    mark = jnp.full((8, 128), p_dir[n][t], jnp.int32) == d
-                    total = jnp.where(mark, parts[t], total)
-                dense.append(total)
-            dense.append(jnp.zeros((8, 128), F32))
-            halves.append(jnp.concatenate(dense, axis=0))
-        dense = jnp.concatenate([halves[0], halves[1][:, :64]], axis=1).astype(BF16)
+        halves = [
+            jnp.concatenate([ps[k, pl.ds(n * 24 + t, 8, stride=4), :] for t in range(SLOTS)], axis=0)
+            for k in range(2)
+        ]
+        own = jnp.concatenate([halves[0], halves[1][:, :64]], axis=1).astype(BF16)
         s_copies[n].wait()
         for s in range(SLOTS):
-            high, low = split(dot(dense, s_buf[n * SLOTS + s]))
-            wb[n, pl.ds(s * 128, 64), :] = high
-            wb[n, pl.ds(s * 128 + 64, 64), :] = low
+            high, low = split(dot(own, s_buf[n * SLOTS + s]))
+            wb[n, pl.ds(s * 64, 32), :] = high
+            wb[n, pl.ds(s * 64 + 32, 32), :] = low
 
     for copy in loads[3:]:
         copy.wait()
@@ -243,52 +241,70 @@
     for arrived, _ in halos:
         arrived()
 
-    lane128 = lax.broadcasted_iota(jnp.int32, (128, 128), 1) // 32
-
-    def term(i, src, dst, d):
-        return exchange(i, src, dst, d, t_s, t_r)
-
-    terms = {}
-    for n in range(NA):
-        x, y = n // AY, n % AY
-        tables, picks = [], []
-        for s in range(SLOTS):
-            e = s_dir[n][s]
-            at = jnp.int32(halo_place(n, 0))
-            for other in range(1, 7):
-                at = jnp.where(e == other, halo_place(n, other), at)
-            table = pm[at // AY, at % AY]
-            tables.append(table[:, :ROWS])
-            code = jnp.broadcast_to(table[:, ROWS:ROWS + 1].astype(F32), (32, 256))
-            wanted = tables_ref[e, :, pl.ds(0, 256)]
-            wanted = jnp.concatenate([wanted] * 4, axis=0)
-            picks.append(jnp.where(code == wanted, 1.0, 0.0).astype(BF16))
-        full = dot_t(wb[n], jnp.concatenate(tables, axis=0))
-        z = jnp.zeros((128, 128), F32)
-        for s in range(SLOTS):
-            z = jnp.where(lane128 == s, full[s * 128:(s + 1) * 128], z)
-        high, low = split(z[:64] + z[64:])
-        both = dot(jnp.concatenate([high, low], axis=0), jnp.concatenate(picks, axis=0))
-        t_all = both[:64] + both[64:]
-        for d, step in enumerate(FACES):
-            block = t_all[d * 8:d * 8 + 8]
-            to_x, to_y = x + step[0], y + step[1]
-            if step[2]:
-                tsz[0 if step[2] < 0 else 1, x, y] = block
-            elif not 0 <= to_x < AX:
-                tsx[0 if step[0] < 0 else 1, y] = block
-            elif not 0 <= to_y < AY:
-                tsy[0 if step[1] < 0 else 1, x] = block
-            else:
-                tbuf[d, to_x, to_y] = block
-        if n == 1:
-            terms[0] = term(0, tsx.at[0], tbuf.at[0, 3], 0)
-        if n == NA - 1:
-            terms[2] = term(1, tsz.at[0], tbuf.at[2], 2)
-            terms[4] = term(2, tsz.at[1], tbuf.at[4], 4)
-            terms[1] = term(3, tsy.at[0], tbuf.at[1, :, 1], 1)
-            terms[5] = term(4, tsy.at[1], tbuf.at[5, :, 0], 5)
-            terms[6] = term(5, tsx.at[1], tbuf.at[6, 0], 6)
+    lane128 = lax.broadcasted_iota(jnp.int32, (64, 128), 1) // 32
+    terms = {d: [] for d in range(7)}
+
+    def term(src, dst, d):
+        i = sum(len(sends) for sends in terms.values())
+        terms[d].append(exchange(i, src, dst, d, t_s, t_r, dst))
+
+    for x in (0, 3, 1, 2):
+        for y in range(AY):
+            n = x * AY + y
+            rows_of, picks = [], []
+            for s in range(SLOTS):
+                e = s_dir[n][s]
+                at = jnp.int32(halo_place(n, 0))
+                for other in range(1, 7):
+                    at = jnp.where(e == other, halo_place(n, other), at)
+                pair, member = at >> 1, at & 1
+                own, shared = pm[pair, 2 * member], pm[pair, 1]
+                rows_of += [own[:, :ROWS], shared[:, :ROWS]]
+                code = jnp.concatenate([own[:, 128:], shared[:, 128:]], axis=0).astype(F32)
+                code = jnp.broadcast_to(code[:, 64:65], (32, 128))
+                keep = lax.broadcasted_iota(jnp.int32, (32, 128), 0) // 8
+                code = jnp.where((keep < 2) | (keep == member + 2), code, -2.0)
+                wanted = tables_ref[e, :, pl.ds(0, 256)]
+                picks.append(
+                    jnp.concatenate(
+                        [
+                            jnp.where(
+                                code == jnp.concatenate([wanted[:, k * 128:k * 128 + 128]] * 4, axis=0), 1.0, 0.0
+                            )
+                            for k in range(2)
+                        ],
+                        axis=1,
+                    ).astype(BF16)
+                )
+            full = dot_t(wb[n], jnp.concatenate(rows_of, axis=0))
+            z = full[:64]
+            for s in range(1, SLOTS):
+                z = jnp.where(lane128 == s, full[s * 64:s * 64 + 64], z)
+            high, low = split(z[:32] + z[32:])
+            both = dot(jnp.concatenate([high, low], axis=0), jnp.concatenate(picks, axis=0))
+            t_all = both[:32] + both[32:]
+            for d, step in enumerate(FACES):
+                block = jnp.zeros((8, 256), F32)
+                for t in range(SLOTS):
+                    mark = jnp.full((8, 256), p_dir[n][t], jnp.int32) == d
+                    block = jnp.where(mark, t_all[t * 8:t * 8 + 8], block)
+                to_x, to_y = x + step[0], y + step[1]
+                if step[2]:
+                    tsz[0 if step[2] < 0 else 1, x, y] = block
+                elif not 0 <= to_x < AX:
+                    tsx[0 if step[0] < 0 else 1, y] = block
+                elif not 0 <= to_y < AY:
+                    tsy[0 if step[1] < 0 else 1, x] = block
+                else:
+                    tbuf[d, to_x, to_y] = block
+        if x == 0:
+            term(tsx.at[0], tbuf.at[0, 3], 0)
+        if x == 3:
+            term(tsx.at[1], tbuf.at[6, 0], 6)
+        term(tsz.at[0, x], tbuf.at[2, x], 2)
+        term(tsz.at[1, x], tbuf.at[4, x], 4)
+        term(tsy.at[0, x], tbuf.at[1, x, 1], 1)
+        term(tsy.at[1, x], tbuf.at[5, x, 0], 5)
 
     def one_hot(source, base):
         wide = source.shape[1]
@@ -303,8 +319,8 @@
 
     total = jnp.zeros((128, 384), F32)
     for d in (3, 0, 6, 1, 5, 2, 4):
-        if d in terms:
-            terms[d][0]()
+        for arrived, _ in terms[d]:
+            arrived()
         high, low = split(tbuf[d].reshape(64, 256))
         total = total + dot(jnp.concatenate([high, low], axis=0), place[d])
     total = total[:64] + total[64:]
@@ -352,7 +368,7 @@
     for copy in sends:
         copy.wait()
     mine.wait()
-    for _, sent in halos + list(terms.values()):
+    for _, sent in halos + sum(terms.values(), []):
         sent()
 
 
@@ -361,9 +377,9 @@
     hbm = pl.BlockSpec(memory_space=pltpu.HBM)
     out = pl.pallas_call(
         functools.partial(kernel, sizes),
-        out_shape=jax.ShapeDtypeStruct((n_gy, CAP, WIDTH), F32),
+        out_shape=pltpu.VMEM((n_gy, CAP, WIDTH), F32),
         in_specs=[hbm] * 7,
-        out_specs=hbm,
+        out_specs=pl.BlockSpec(memory_space=pltpu.VMEM),
         scratch_shapes=[
             pltpu.VMEM((NA, MODES, SLOTS, ROWS), BF16),
             pltpu.SMEM(stiff_cols.shape, jnp.int32),
@@ -374,9 +390,9 @@
             pltpu.VMEM((NA * SLOTS, ROWS, ROWS), BF16),
             pltpu.VMEM((7, 256, 384), BF16),
             pltpu.VMEM((MODES * 128, MODES * 128), BF16),
-            pltpu.VMEM((2, NA * 32, 128), F32),
-            pltpu.VMEM((18, AY, 32, 256), BF16),
-            pltpu.VMEM((NA, 512, ROWS), BF16),
+            pltpu.VMEM((2, NA * 24 + 8, 128), F32),
+            pltpu.VMEM((22, 3, 16, 256), BF16),
+            pltpu.VMEM((NA, 256, ROWS), BF16),
             pltpu.VMEM((7, AX, AY, 8, 256), F32),
             pltpu.VMEM((2, AY, 8, 256), F32),
             pltpu.VMEM((2, AX, 8, 256), F32),
@@ -386,16 +402,16 @@
             pltpu.VMEM((n_gy, CAP, WIDTH), F32),
             pltpu.SemaphoreType.DMA((6,)),
             pltpu.SemaphoreType.DMA((NA,)),
-            pltpu.SemaphoreType.DMA((8,)),
-            pltpu.SemaphoreType.DMA((8,)),
             pltpu.SemaphoreType.DMA((6,)),
             pltpu.SemaphoreType.DMA((6,)),
+            pltpu.SemaphoreType.DMA((18,)),
+            pltpu.SemaphoreType.DMA((18,)),
             pltpu.SemaphoreType.DMA((n_gy - 1,)),
             pltpu.SemaphoreType.DMA((n_gy - 1,)),
             pltpu.SemaphoreType.DMA,
         ],
         compiler_params=pltpu.CompilerParams(
-            collective_id=0, has_side_effects=True, vmem_limit_bytes=62 * 1024 * 1024
+            collective_id=0, has_side_effects=True, vmem_limit_bytes=60 * 1024 * 1024
         ),
         name="galerkin",
     )(

time: 34.1 us -> 31.9 us (0.935)
  Pallas kernels: 32.3 us -> 31.1 us
  local copies, waits for them, and re-layouts: 1.58 us -> 0.66 us
    pallas_call x1, Pallas kernels: 32.3 us -> 31.1 us  [local(): pl.pallas_call(functools.partial(kernel, sizes), out_shape=pltpu.VMEM((n_...]
    unnamed x1, local copies, waits for them, and re-layouts: 1.58 us -> 0.66 us
where the time goes in v3:
time: 31.9 us; the launch traced here: 31.8 us
  Pallas kernels  31.1 us (97%)
  local copies, waits for them, and re-layouts  0.66 us (2%)
    pallas_call x1, Pallas kernels, local(): pl.pallas_call(functools.partial(kernel, sizes), out_shape=pltpu.VMEM((n_...  31.1 us
    unnamed x1, local copies, waits for them, and re-layouts  0.66 us

profile of v3, /device:TPU:1, one launch (start us, length us, event | category | flops | bytes accessed | tf_op | source)
XLA Modules:
  0.0 31.8 jit_solution(14624786812815002640)
XLA Ops:
  0.0 31.1 %galerkin.1 = f32[8,2,2268]{2,1,0:T(2,128)S(1)} custom-call(bf16[8,6,4,192]{3,2,1,0:T(4,128)(2,1)} %bitcast.13, s32[4,2,1,4]{3,2,1,0:T(1,128)} %scols_hbm.1, s32[4,2,1,4]{3,2,1,0:T(1,128)} %pcols_hbm.1, s32[2,1,4]{2,1,0:T(1,128)} %bitcast.15, s32[1,8,1,1,8]{4,3,2,1,0:T(1,128)} %bitcast.14, f32[8,8,768]{2,1,0:T(8,128)} %constant.2.clone.tables_hbm, ...), custom_call_target="tpu_custom_call" | custom-call | tf_op jit(solution)/shard_map/galerkin/pallas_call | solution.py:378
  31.1 0.7 %copy.11 = f32[1,8,1,2,2268]{4,3,2,1,0:T(2,128)} copy(f32[1,8,1,2,2268]{4,3,2,1,0:T(2,128)S(1)} %bitcast.11) | data formatting | bytes 290304

commit v4 on v3

--- a/solution.py
+++ b/solution.py
@@ -87,7 +87,7 @@
     out,
     p_ref, scols, pcols, nodes, owners, tables_ref,
     s_buf, place, order, ps, pm, wb, tbuf, tsx, tsy, tsz, xs, rows, sbuf,
-    in_sem, s_sem, ph_s, ph_r, t_s, t_r, o_s, o_r, own_sem,
+    in_sem, s_sem, ph_s, ph_r, t_s, t_r, o_s, o_r,
 ):
     n_gx, n_gy, n_gz = sizes
     gx, gy, gz = lax.axis_index("gx"), lax.axis_index("gy"), lax.axis_index("gz")
@@ -348,26 +348,25 @@
             rank = rank + (owner[other] == owner[q]).astype(jnp.int32)
         spot.append(owner[q] * CAP + rank)
     row2 = lax.broadcasted_iota(jnp.int32, (CAP, WIDTH), 0)
-    for target in range(n_gy):
+    sends = []
+    for r in sorted(range(n_gy), key=lambda r: -min(r, n_gy - r)):
+        target = lax.rem(gy + r, n_gy)
         chosen = jnp.zeros((CAP, WIDTH), F32)
         for q in range(NA):
             row = jnp.broadcast_to(rows[pl.ds(q, 1), pl.ds(0, WIDTH)], (CAP, WIDTH))
             chosen = jnp.where(row2 + target * CAP == spot[q], row, chosen)
-        sbuf[target] = chosen
-    sends = []
-    for r in range(1, n_gy):
-        target = lax.rem(gy + r, n_gy)
+        if r == 0:
+            out[gy] = chosen
+            continue
+        sbuf[r] = chosen
         copy = pltpu.make_async_remote_copy(
-            src_ref=sbuf.at[target], dst_ref=out.at[gy], send_sem=o_s.at[r - 1], recv_sem=o_r.at[r - 1],
+            src_ref=sbuf.at[r], dst_ref=out.at[gy], send_sem=o_s.at[r - 1], recv_sem=o_r.at[r - 1],
             device_id={"gy": target}, device_id_type=MESH,
         )
         copy.start()
         sends.append(copy)
-    mine = pltpu.make_async_copy(sbuf.at[gy], out.at[gy], own_sem)
-    mine.start()
     for copy in sends:
         copy.wait()
-    mine.wait()
     for _, sent in halos + sum(terms.values(), []):
         sent()
 
@@ -408,7 +407,6 @@
             pltpu.SemaphoreType.DMA((18,)),
             pltpu.SemaphoreType.DMA((n_gy - 1,)),
             pltpu.SemaphoreType.DMA((n_gy - 1,)),
-            pltpu.SemaphoreType.DMA,
         ],
         compiler_params=pltpu.CompilerParams(
             collective_id=0, has_side_effects=True, vmem_limit_bytes=60 * 1024 * 1024

time: 31.9 us -> 31.4 us (0.984)
  Pallas kernels: 31.1 us -> 30.6 us
    pallas_call x1, Pallas kernels: 31.1 us -> 30.6 us  [local(): pl.pallas_call(functools.partial(kernel, sizes), out_shape=pltpu.VMEM((n_...]
where the time goes in v4:
time: 31.4 us; the launch traced here: 31.3 us
  Pallas kernels  30.6 us (97%)
  local copies, waits for them, and re-layouts  0.66 us (2%)
    pallas_call x1, Pallas kernels, local(): pl.pallas_call(functools.partial(kernel, sizes), out_shape=pltpu.VMEM((n_...  30.6 us
    unnamed x1, local copies, waits for them, and re-layouts  0.66 us

profile of v4, /device:TPU:1, one launch (start us, length us, event | category | flops | bytes accessed | tf_op | source)
XLA Modules:
  0.0 31.3 jit_solution(4204522697669456010)
XLA Ops:
  0.0 30.6 %galerkin.1 = f32[8,2,2268]{2,1,0:T(2,128)S(1)} custom-call(bf16[8,6,4,192]{3,2,1,0:T(4,128)(2,1)} %bitcast.13, s32[4,2,1,4]{3,2,1,0:T(1,128)} %scols_hbm.1, s32[4,2,1,4]{3,2,1,0:T(1,128)} %pcols_hbm.1, s32[2,1,4]{2,1,0:T(1,128)} %bitcast.15, s32[1,8,1,1,8]{4,3,2,1,0:T(1,128)} %bitcast.14, f32[8,8,768]{2,1,0:T(8,128)} %constant.2.clone.tables_hbm, ...), custom_call_target="tpu_custom_call" | custom-call | tf_op jit(solution)/shard_map/galerkin/pallas_call | solution.py:377
  30.6 0.7 %copy.11 = f32[1,8,1,2,2268]{4,3,2,1,0:T(2,128)} copy(f32[1,8,1,2,2268]{4,3,2,1,0:T(2,128)S(1)} %bitcast.11) | data formatting | bytes 290304

commit v5 on v4

--- a/solution.py
+++ b/solution.py
@@ -228,9 +228,7 @@
         own = jnp.concatenate([halves[0], halves[1][:, :64]], axis=1).astype(BF16)
         s_copies[n].wait()
         for s in range(SLOTS):
-            high, low = split(dot(own, s_buf[n * SLOTS + s]))
-            wb[n, pl.ds(s * 64, 32), :] = high
-            wb[n, pl.ds(s * 64 + 32, 32), :] = low
+            wb[n, pl.ds(s * 32, 32), :] = dot(own, s_buf[n * SLOTS + s]).astype(BF16)
 
     for copy in loads[3:]:
         copy.wait()
@@ -241,7 +239,7 @@
     for arrived, _ in halos:
         arrived()
 
-    lane128 = lax.broadcasted_iota(jnp.int32, (64, 128), 1) // 32
+    lane128 = lax.broadcasted_iota(jnp.int32, (32, 128), 1) // 32
     terms = {d: [] for d in range(7)}
 
     def term(src, dst, d):
@@ -277,10 +275,10 @@
                     ).astype(BF16)
                 )
             full = dot_t(wb[n], jnp.concatenate(rows_of, axis=0))
-            z = full[:64]
+            z = full[:32]
             for s in range(1, SLOTS):
-                z = jnp.where(lane128 == s, full[s * 64:s * 64 + 64], z)
-            high, low = split(z[:32] + z[32:])
+                z = jnp.where(lane128 == s, full[s * 32:s * 32 + 32], z)
+            high, low = split(z)
             both = dot(jnp.concatenate([high, low], axis=0), jnp.concatenate(picks, axis=0))
             t_all = both[:32] + both[32:]
             for d, step in enumerate(FACES):
@@ -391,7 +389,7 @@
             pltpu.VMEM((MODES * 128, MODES * 128), BF16),
             pltpu.VMEM((2, NA * 24 + 8, 128), F32),
             pltpu.VMEM((22, 3, 16, 256), BF16),
-            pltpu.VMEM((NA, 256, ROWS), BF16),
+            pltpu.VMEM((NA, 128, ROWS), BF16),
             pltpu.VMEM((7, AX, AY, 8, 256), F32),
             pltpu.VMEM((2, AY, 8, 256), F32),
             pltpu.VMEM((2, AX, 8, 256), F32),

time: 31.4 us -> 31.1 us (level)
  Pallas kernels: 30.6 us -> 30.2 us
    pallas_call x1, Pallas kernels: 30.6 us -> 30.2 us  [local(): pl.pallas_call(functools.partial(kernel, sizes), out_shape=pltpu.VMEM((n_...]
where the time goes in v5:
time: 31.1 us; the launch traced here: 30.9 us
  Pallas kernels  30.2 us (97%)
  local copies, waits for them, and re-layouts  0.66 us (2%)
    pallas_call x1, Pallas kernels, local(): pl.pallas_call(functools.partial(kernel, sizes), out_shape=pltpu.VMEM((n_...  30.2 us
    unnamed x1, local copies, waits for them, and re-layouts  0.66 us

profile of v5, /device:TPU:1, one launch (start us, length us, event | category | flops | bytes accessed | tf_op | source)
XLA Modules:
  0.0 30.9 jit_solution(11998536235172125150)
XLA Ops:
  0.0 30.2 %galerkin.1 = f32[8,2,2268]{2,1,0:T(2,128)S(1)} custom-call(bf16[8,6,4,192]{3,2,1,0:T(4,128)(2,1)} %bitcast.13, s32[4,2,1,4]{3,2,1,0:T(1,128)} %scols_hbm.1, s32[4,2,1,4]{3,2,1,0:T(1,128)} %pcols_hbm.1, s32[2,1,4]{2,1,0:T(1,128)} %bitcast.15, s32[1,8,1,1,8]{4,3,2,1,0:T(1,128)} %bitcast.14, f32[8,8,768]{2,1,0:T(8,128)} %constant.2.clone.tables_hbm, ...), custom_call_target="tpu_custom_call" | custom-call | tf_op jit(solution)/shard_map/galerkin/pallas_call | solution.py:375
  30.2 0.7 %copy.11 = f32[1,8,1,2,2268]{4,3,2,1,0:T(2,128)} copy(f32[1,8,1,2,2268]{4,3,2,1,0:T(2,128)S(1)} %bitcast.11) | data formatting | bytes 290304

commit v6 on v5

--- a/solution.py
+++ b/solution.py
@@ -246,8 +246,8 @@
         i = sum(len(sends) for sends in terms.values())
         terms[d].append(exchange(i, src, dst, d, t_s, t_r, dst))
 
-    for x in (0, 3, 1, 2):
-        for y in range(AY):
+    for first, second in ((0, 3), (1, 2)):
+        for x, y in ((first, 0), (first, 1), (second, 0), (second, 1)):
             n = x * AY + y
             rows_of, picks = [], []
             for s in range(SLOTS):
@@ -295,14 +295,15 @@
                     tsy[0 if step[1] < 0 else 1, x] = block
                 else:
                     tbuf[d, to_x, to_y] = block
-        if x == 0:
-            term(tsx.at[0], tbuf.at[0, 3], 0)
-        if x == 3:
-            term(tsx.at[1], tbuf.at[6, 0], 6)
-        term(tsz.at[0, x], tbuf.at[2, x], 2)
-        term(tsz.at[1, x], tbuf.at[4, x], 4)
-        term(tsy.at[0, x], tbuf.at[1, x, 1], 1)
-        term(tsy.at[1, x], tbuf.at[5, x, 0], 5)
+        for x in (first, second):
+            if x == 0:
+                term(tsx.at[0], tbuf.at[0, 3], 0)
+            if x == 3:
+                term(tsx.at[1], tbuf.at[6, 0], 6)
+            term(tsz.at[0, x], tbuf.at[2, x], 2)
+            term(tsz.at[1, x], tbuf.at[4, x], 4)
+            term(tsy.at[0, x], tbuf.at[1, x, 1], 1)
+            term(tsy.at[1, x], tbuf.at[5, x, 0], 5)
 
     def one_hot(source, base):
         wide = source.shape[1]

time: 31.1 us -> 30.8 us (level)
  no operation moved by 1% of the time
where the time goes in v6:
time: 30.8 us; the launch traced here: 30.6 us
  Pallas kernels  29.9 us (97%)
  local copies, waits for them, and re-layouts  0.66 us (2%)
    pallas_call x1, Pallas kernels, local(): pl.pallas_call(functools.partial(kernel, sizes), out_shape=pltpu.VMEM((n_...  29.9 us
    unnamed x1, local copies, waits for them, and re-layouts  0.66 us

profile of v6, /device:TPU:1, one launch (start us, length us, event | category | flops | bytes accessed | tf_op | source)
XLA Modules:
  0.0 30.6 jit_solution(2377528970076413458)
XLA Ops:
  0.0 29.9 %galerkin.1 = f32[8,2,2268]{2,1,0:T(2,128)S(1)} custom-call(bf16[8,6,4,192]{3,2,1,0:T(4,128)(2,1)} %bitcast.13, s32[4,2,1,4]{3,2,1,0:T(1,128)} %scols_hbm.1, s32[4,2,1,4]{3,2,1,0:T(1,128)} %pcols_hbm.1, s32[2,1,4]{2,1,0:T(1,128)} %bitcast.15, s32[1,8,1,1,8]{4,3,2,1,0:T(1,128)} %bitcast.14, f32[8,8,768]{2,1,0:T(8,128)} %constant.2.clone.tables_hbm, ...), custom_call_target="tpu_custom_call" | custom-call | tf_op jit(solution)/shard_map/galerkin/pallas_call | solution.py:376
  29.9 0.7 %copy.11 = f32[1,8,1,2,2268]{4,3,2,1,0:T(2,128)} copy(f32[1,8,1,2,2268]{4,3,2,1,0:T(2,128)S(1)} %bitcast.11) | data formatting | bytes 290304
